TPU v7x, 1024 devices: a whole 8x8x8 slice. The times are simulated.
1024 devices in a mesh: tbl: 64 (over y, x), rep: 16 (over z, core).
Axes of the slice: x: 8, y: 8, z: 8, core: 2. Of those that a mesh axis runs over, the one named last changes fastest.
Arguments:
- x_zero: bfloat16 [4096, 24576], P('rep', 'tbl'), may hold values from -6 to 6
- grad_top: bfloat16 [4096, 24576], P('rep', 'tbl'), may hold values from -0.5 to 0.5
- low_zero: bfloat16 [4096, 512], P('rep'), may hold values from -6 to 6
- low_one: bfloat16 [4096, 512], P('rep'), may hold values from -6 to 6
- lift_zero: bfloat16 [512, 24576], P(None, 'tbl'), may hold values from -0.25 to 0.25
- lift_one: bfloat16 [512, 24576], P(None, 'tbl'), may hold values from -0.25 to 0.25
- squeeze_zero: bfloat16 [24576, 512], P('tbl'), may hold values from -0.0390625 to 0.0390625
- squeeze_one: bfloat16 [24576, 512], P('tbl'), may hold values from -0.0390625 to 0.0390625
- bias_zero: float32 [24576], P('tbl'), may hold values from -3 to 3
- bias_one: float32 [24576], P('tbl'), may hold values from -3 to 3
- table_owner: int32 [384], replicated, may hold values from 0 to 63, as said below
- table_slot: int32 [384], replicated, may hold values from 0 to 17
- incidence: int32 [1152, 4096, 128], P('tbl', 'rep'), may hold values 0 or 1
- table_rows: float32 [1152, 8192], P('tbl'), may hold values from -1.5 to 1.5
- row_accum: float32 [1152, 128], P('tbl'), may hold values from 0.1 to 4
Outputs:
- new_rows: float32 [1152, 8192], P('tbl')
- new_accum: float32 [1152, 128], P('tbl')
Inputs may be any that keep to these rules, and one draw needn't show every extreme that they name: `table_owner`: no two tables have the same owner and slot; an owner's tables fill its slots from 0 upward; every owner holds 2 or 18 tables, the larger count on a quarter of the owners; an owner holds at most 1 of the tables t with the same t // 6, and some owner holds exactly that many.
All inputs are finite; a program needn't handle non-finite values. No bound on the sum of `incidence` on one device may be relied on, other than what follows from the above.
Results may differ from a plain program's by a relative error of at most 0.0035.
Values may be sent and summed in bfloat16 or wider, within the bound.
No kernel may reach another device: no remote copies, remote signals or barrier semaphores. Data moves between devices by JAX's collectives and lax.ppermute only.
A program may use at most 32 MiB of HBM per device.

v0:
```python
import jax
import jax.numpy as jnp
from jax import lax
from jax.sharding import PartitionSpec as P

FEATS = 384
EMB = 64


LEARN_RATE = 0.25
EPSILON = 1e-06


def rank_sum(scaled, lift):
    local_part = lax.dot_general(
        scaled, lift, (((1,), (1,)), ((), ())), preferred_element_type=jnp.float32
    )
    return lax.psum(local_part, "tbl").astype(jnp.bfloat16)


def widen_rank(rank_part, squeeze):
    return lax.dot_general(
        rank_part, squeeze, (((1,), (1,)), ((), ())), preferred_element_type=jnp.float32
    )


def adagrad(gradient, current, history):
    history_new = history + jnp.mean(gradient * gradient, axis=2)
    current_new = current - LEARN_RATE * gradient / (jnp.sqrt(history_new)[:, :, None] + EPSILON)
    return (current_new, history_new)


def shards(
    x_zero,
    grad_top,
    low_zero,
    low_one,
    lift_zero,
    lift_one,
    squeeze_zero,
    squeeze_one,
    bias_zero,
    bias_one,
    table_owner,
    table_slot,
    incidence,
    table_rows,
    row_accum,
):
    upstream = grad_top.astype(jnp.float32)
    embedded = x_zero.astype(jnp.float32)
    gate_one = jnp.dot(low_one, lift_one, preferred_element_type=jnp.float32) + bias_one
    gate_zero = jnp.dot(low_zero, lift_zero, preferred_element_type=jnp.float32) + bias_zero
    rank_one = rank_sum((upstream * embedded).astype(jnp.bfloat16), lift_one)
    grad_mid = upstream + widen_rank(rank_one, squeeze_one)
    rank_zero = rank_sum((grad_mid * embedded).astype(jnp.bfloat16), lift_zero)
    pooled = (
        upstream * gate_one + grad_mid * gate_zero + grad_mid + widen_rank(rank_zero, squeeze_zero)
    ).astype(jnp.bfloat16)
    devices = lax.axis_size("tbl")
    slot_count = incidence.shape[0]
    touched = incidence.shape[2]
    by_rows = lax.all_to_all(pooled, "tbl", split_axis=0, concat_axis=1, tiled=True)
    few_rows = by_rows.shape[0]
    wanted = jnp.arange(devices * slot_count, dtype=jnp.int32)
    placed = table_owner * slot_count + table_slot
    matches = placed[None, :] == wanted[:, None]
    table_of = jnp.sum(jnp.where(matches, jnp.arange(FEATS, dtype=jnp.int32)[None, :], 0), axis=1)
    occupied = jnp.any(matches, axis=1)
    spread = by_rows.reshape(few_rows, FEATS, EMB)
    picked = jnp.where(
        occupied[None, :, None], jnp.take(spread, table_of, axis=1), jnp.zeros((), jnp.bfloat16)
    )
    outgoing = jnp.transpose(picked, (1, 0, 2)).reshape(devices, slot_count, few_rows * EMB)
    arrived = lax.all_to_all(outgoing, "tbl", split_axis=0, concat_axis=0, tiled=True)
    arrived = arrived.reshape(devices, slot_count, few_rows, EMB)
    incident = incidence.astype(jnp.bfloat16).reshape(slot_count, devices, few_rows, touched)
    partial_value = jnp.einsum(
        "snru,nsre->sue", incident, arrived, preferred_element_type=jnp.float32
    )
    rows_now = table_rows.reshape(slot_count, touched, EMB)
    summed = lax.psum(partial_value, "rep")
    rows_new, history_new = adagrad(summed, rows_now, row_accum)
    return (rows_new.reshape(slot_count, touched * EMB), history_new)


def solution(mesh):
    in_specs = (
        P("rep", "tbl"),
        P("rep", "tbl"),
        P("rep", None),
        P("rep", None),
        P(None, "tbl"),
        P(None, "tbl"),
        P("tbl", None),
        P("tbl", None),
        P("tbl"),
        P("tbl"),
        P(),
        P(),
        P("tbl", "rep", None),
        P("tbl", None),
        P("tbl", None),
    )
    out_specs = (P("tbl", None), P("tbl", None))
    return jax.shard_map(shards, mesh=mesh, in_specs=in_specs, out_specs=out_specs, check_vma=False)
```

profile of v0, /device:TPU:1, one launch (start us, length us, event | category | flops | bytes accessed | tf_op | source)
XLA Modules:
  0.0 766.5 jit_solution(12157736530199504374)
XLA Ops:
  7.2 0.0 copy-start
  7.2 1.6 fusion.11
  8.8 0.0 copy-start.3
  8.8 229.0 %all-reduce.5 = bf16[256,512]{1,0:T(8,128)(2,1)S(1)} all-reduce(f32[256,512]{1,0:T(8,128)S(1)} %fusion.11), channel_id=1, replica_groups=mesh['tbl'=64,'rep'=16] {'tbl'}, use_global_device_ids=true, to_apply=%region_2.3 | all-reduce | flops 131072 | bytes 786432 | tf_op jit(solution)/shard_map/psum | solution.py:18
  237.8 0.3 convolution_add_fusion.2
  238.1 0.0 copy-done
  238.1 0.0 copy-done.3
  238.2 0.0 copy-start.7
  238.2 0.0 copy-start.9
  238.2 0.3 fusion.13
  238.5 0.0 copy-start.2
  238.5 0.0 copy-start.6
  238.5 0.0 copy-start.10
  238.6 222.1 %all-reduce.6 = bf16[256,512]{1,0:T(8,128)(2,1)S(1)} all-reduce(f32[256,512]{1,0:T(8,128)S(1)} %fusion.13), channel_id=1, replica_groups=mesh['tbl'=64,'rep'=16] {'tbl'}, use_global_device_ids=true, to_apply=%region_3.4 | all-reduce | flops 131072 | bytes 786432 | tf_op jit(solution)/shard_map/psum | solution.py:18
  460.7 0.3 fusion.4
  461.0 0.0 copy-done.2
  461.0 0.0 copy-done.6
  461.0 0.0 copy-done.10
  461.0 0.0 copy-start.5
  461.0 0.3 fusion.3
  461.3 0.7 copy-done.5
  462.0 0.3 fusion.6
  462.3 0.7 all_to_all.15
  463.1 4.7 all-to-all-start
  467.8 0.3 select_reduce_fusion
  468.1 0.3 fusion
  468.4 11.4 %all-to-all-done = bf16[64,4,384]{2,1,0:T(4,128)(2,1)S(1)} async-done(((bf16[64,4,384]{2,1,0:T(4,128)(2,1)}), bf16[64,4,384]{2,1,0:T(4,128)(2,1)S(1)}, u32[]{:S(2)}, u32[]{:S(2)}) %all-to-all-start) | async-done | bytes 196640 | tf_op jit(solution)/shard_map/all_to_all | solution.py:63
  479.8 0.2 reshape.51
  480.0 0.3 copy.31
  480.4 4.3 gather_fusion
  484.7 5.6 select_select_fusion
  490.3 1.8 reshape.52
  492.1 4.6 all-to-all-start.1
  496.8 0.0 all-reduce.4.cloned.1.call-start
  496.8 1.9 convert_element_type.31
  498.7 14.8 %all-to-all-done.1 = bf16[64,18,256]{2,1,0:T(8,128)(2,1)S(1)} async-done(((bf16[64,18,256]{2,1,0:T(8,128)(2,1)}), bf16[64,18,256]{2,1,0:T(8,128)(2,1)S(1)}, u32[]{:S(2)}, u32[]{:S(2)}) %all-to-all-start.1) | async-done | bytes 589856 | tf_op jit(solution)/shard_map/all_to_all | solution.py:75
  513.5 0.8 copy.32
  514.4 1.3 convolution_bitcast_fusion
  515.7 0.0 all-reduce.4.cloned.1.call-update
  515.7 1.6 reshape.50
  517.3 0.0 copy-start.8
  517.3 0.3 copy.34
  517.7 237.4 %all-reduce.4.cloned.1.call-done = f32[18,128,64]{1,2,0:T(8,128)} async-done(((f32[18,128,64]{1,2,0:T(8,128)}), f32[18,128,64]{1,2,0:T(8,128)}) %all-reduce.4.cloned.1.call-update) | async-done | bytes 589840 | tf_op jit(solution)/shard_map/psum | solution.py:82
  755.1 1.1 multiply_reduce_fusion
  756.3 0.6 sqrt_add_fusion
  756.9 1.1 divide_subtract_fusion
  758.0 0.4 copy.35
  758.4 1.3 reshape.55
  (16 shorter events, 0.1 us)
Async XLA Ops:
  7.2 231.0 %copy-start = (bf16[512,384]{1,0:T(8,128)(2,1)S(1)}, bf16[512,384]{1,0:T(8,128)(2,1)}, u32[]{:S(2)}) copy-start(bf16[512,384]{1,0:T(8,128)(2,1)} %param.19) | copy-start | bytes 1179652
  7.2 230.6 %copy-start.1 = (bf16[256,384]{1,0:T(8,128)(2,1)S(1)}, bf16[256,384]{1,0:T(8,128)(2,1)}, u32[]{:S(2)}) copy-start(bf16[256,384]{1,0:T(8,128)(2,1)} %param.16) | copy-start | bytes 589828
  7.2 230.6 %copy-start.4 = (bf16[384,512]{1,0:T(8,128)(2,1)S(1)}, bf16[384,512]{1,0:T(8,128)(2,1)}, u32[]{:S(2)}) copy-start(bf16[384,512]{1,0:T(8,128)(2,1)} %param.22) | copy-start | bytes 1179652
  8.8 229.3 %copy-start.3 = (bf16[256,384]{1,0:T(8,128)(2,1)S(1)}, bf16[256,384]{1,0:T(8,128)(2,1)}, u32[]{:S(2)}) copy-start(bf16[256,384]{1,0:T(8,128)(2,1)} %param.15) | copy-start | bytes 589828
  238.2 222.5 %copy-start.7 = (bf16[256,512]{1,0:T(8,128)(2,1)S(1)}, bf16[256,512]{1,0:T(8,128)(2,1)}, u32[]{:S(2)}) copy-start(bf16[256,512]{1,0:T(8,128)(2,1)} %param.17) | copy-start | bytes 786436
  238.2 222.5 %copy-start.9 = (f32[384]{0:T(512)S(1)}, f32[384]{0:T(512)}, u32[]{:S(2)}) copy-start(f32[384]{0:T(512)} %param.23) | copy-start | bytes 4612
  238.5 222.5 %copy-start.2 = (bf16[512,384]{1,0:T(8,128)(2,1)S(1)}, bf16[512,384]{1,0:T(8,128)(2,1)}, u32[]{:S(2)}) copy-start(bf16[512,384]{1,0:T(8,128)(2,1)} %param.20) | copy-start | bytes 1179652
  238.5 222.4 %copy-start.6 = (bf16[256,512]{1,0:T(8,128)(2,1)S(1)}, bf16[256,512]{1,0:T(8,128)(2,1)}, u32[]{:S(2)}) copy-start(bf16[256,512]{1,0:T(8,128)(2,1)} %param.18) | copy-start | bytes 786436
  238.5 222.4 %copy-start.10 = (f32[384]{0:T(512)S(1)}, f32[384]{0:T(512)}, u32[]{:S(2)}) copy-start(f32[384]{0:T(512)} %param.24) | copy-start | bytes 4612
  461.0 1.0 copy-start.5
  462.0 5.8 copy-start.11
  462.0 5.8 copy-start.12
  463.1 16.7 %all-to-all-start = ((bf16[64,4,384]{2,1,0:T(4,128)(2,1)}), bf16[64,4,384]{2,1,0:T(4,128)(2,1)S(1)}, u32[]{:S(2)}, u32[]{:S(2)}) async-start(bf16[64,4,384]{2,1,0:T(4,128)(2,1)} %all_to_all.15), calls=%async_computation | async-start | bytes 393216 | tf_op jit(solution)/shard_map/all_to_all | solution.py:63
  492.1 21.4 %all-to-all-start.1 = ((bf16[64,18,256]{2,1,0:T(8,128)(2,1)}), bf16[64,18,256]{2,1,0:T(8,128)(2,1)S(1)}, u32[]{:S(2)}, u32[]{:S(2)}) async-start(bf16[64,18,256]{2,1,0:T(8,128)(2,1)} %reshape.52), calls=%async_computation.1 | async-start | bytes 1572864 | tf_op jit(solution)/shard_map/all_to_all | solution.py:75
  496.8 258.4 %all-reduce.4.cloned.1.call-start = ((), (), s32[]{:S(2)}) async-start(), calls=%async_computation.2 | async-start | bytes 1179648 | tf_op jit(solution)/shard_map/psum | solution.py:82
  517.3 238.9 %copy-start.8 = (f32[18,128]{1,0:T(8,128)S(1)}, f32[18,128]{1,0:T(8,128)}, u32[]{:S(2)}) copy-start(f32[18,128]{1,0:T(8,128)} %param.29) | copy-start | bytes 27652
Sparse Core Ops, SparseCore 0:
  515.8 239.2 all-reduce.3
where the time goes:
time: 767 us
  blocking collectives  451 us (59%)
  waiting for transfers between devices  264 us (34%)
  between operations  14.4 us (2%)
  local copies, waits for them, and re-layouts  12.6 us (2%)
  other arithmetic  11 us (1%)
  starting transfers between devices  9.4 us (1%)
    psum x2, blocking collectives, rank_sum(): return lax.psum(local_part, 'tbl').astype(jnp.bfloat16)  451 us
    psum x1, waiting for transfers between devices, shards(): summed = lax.psum(partial_value, 'rep')  237 us
  transfers between devices with their start and end apart: 3, of which 3 were waited for; matrix products, arithmetic and copies ran while one was open for 1% of the time, Pallas kernels for 0%

commit v1 on v0

v1 whole, which is shorter than its diff:
```python
import jax
import jax.numpy as jnp
from jax import lax
from jax.sharding import Mesh, PartitionSpec as P

FEATS = 384
EMB = 64
RANK = 512
ROWS = 256
TOUCH = 128
SLOT_MAX = 18
SLOT_PAD = 24
N_TBL = 64
N_REP = 16
PER_DEV = FEATS // N_TBL

LEARN_RATE = 0.25
EPSILON = 1e-06

TBL = ("y", "x")
REP = ("z", "core")
BF16 = jnp.bfloat16
F32 = jnp.float32


def exchange(blocks, axis):
    return lax.all_to_all(blocks, axis, split_axis=0, concat_axis=0, tiled=True)


def to_tiles(matrix):
    return matrix.reshape(16, 16, 4, 128).transpose(0, 2, 1, 3).reshape(64, 16, 128)


def from_tiles(tiles):
    return tiles.reshape(16, 4, 16, 128).transpose(0, 2, 1, 3).reshape(ROWS, RANK)


def shards(
    x_zero,
    grad_top,
    low_zero,
    low_one,
    lift_zero,
    lift_one,
    squeeze_zero,
    squeeze_one,
    bias_zero,
    bias_one,
    table_owner,
    table_slot,
    incidence,
    table_rows,
    row_accum,
):
    me = lax.axis_index(TBL)
    rep = lax.axis_index(REP)
    core = lax.axis_index("core")
    upstream = grad_top.astype(F32)
    embedded = x_zero.astype(F32)

    tile_rows, tile_cols = rep // 4, rep % 4
    tiles = lax.dynamic_slice(
        squeeze_zero.reshape(PER_DEV, EMB, RANK), (0, tile_rows * 16, tile_cols * 128), (PER_DEV, 16, 128)
    )
    my_owner = lax.dynamic_slice(table_owner, (me * PER_DEV,), (PER_DEV,))
    chosen = (my_owner[None, :] == jnp.arange(N_TBL)[:, None]).astype(BF16)
    squeeze_send = jnp.einsum("ot,trl->orl", chosen, tiles, preferred_element_type=F32).astype(BF16)

    part_one = lax.dot_general(
        (upstream * embedded).astype(BF16), lift_one, (((1,), (1,)), ((), ())), preferred_element_type=F32
    ).astype(BF16)
    got = exchange(jnp.concatenate([to_tiles(part_one), squeeze_send], axis=1), TBL)
    rank_tile = jnp.sum(got[:, :16].astype(F32), axis=0).astype(BF16)
    rank_one = from_tiles(exchange(jnp.broadcast_to(rank_tile[None], (N_TBL, 16, 128)), TBL))

    from_me = (table_owner == me)[None, :] & (table_slot[None, :] == jnp.arange(SLOT_MAX)[:, None])
    source = jnp.any(from_me.reshape(SLOT_MAX, N_TBL, PER_DEV), axis=2).astype(BF16)
    squeeze_slots = jnp.einsum("si,irl->srl", source, got[:, 16:], preferred_element_type=F32).astype(BF16)
    squeeze_all = lax.all_gather(squeeze_slots.reshape(SLOT_MAX * 16, 128), REP, axis=0, tiled=True)
    squeeze_own = (
        squeeze_all.reshape(4, 4, SLOT_MAX, 16, 128).transpose(2, 0, 3, 1, 4).reshape(SLOT_MAX * EMB, RANK)
    )

    gate_one = jnp.dot(low_one, lift_one, preferred_element_type=F32) + bias_one
    gate_zero = jnp.dot(low_zero, lift_zero, preferred_element_type=F32) + bias_zero
    grad_mid = upstream + lax.dot_general(
        rank_one, squeeze_one, (((1,), (1,)), ((), ())), preferred_element_type=F32
    )
    part_zero = lax.dot_general(
        (grad_mid * embedded).astype(BF16), lift_zero, (((1,), (1,)), ((), ())), preferred_element_type=F32
    ).astype(BF16)
    pooled_local = (upstream * gate_one + grad_mid * gate_zero + grad_mid).astype(BF16)
    by_column = pooled_local.reshape(2, 128, PER_DEV, EMB).transpose(3, 0, 2, 1)
    by_column = jnp.pad(by_column, ((0, 0), (0, 0), (0, 8 - PER_DEV), (0, 0))).reshape(N_TBL, 16, 128)
    got = exchange(jnp.concatenate([to_tiles(part_zero), by_column], axis=1), TBL)
    rank_tile = jnp.sum(got[:, :16].astype(F32), axis=0).astype(BF16)

    place = jnp.pad(
        (table_owner * SLOT_PAD + table_slot).reshape(N_TBL, PER_DEV), ((0, 0), (0, 8 - PER_DEV)), constant_values=-1
    ).reshape(-1)
    wanted = (jnp.arange(N_TBL * SLOT_PAD)[:, None] == place[None, :]).astype(BF16)
    halves = got[:, 16:].reshape(N_TBL, 2, 8, 128).transpose(1, 0, 2, 3).reshape(2, N_TBL * 8, 128)
    placed = jnp.einsum("qk,hkb->qhb", wanted, halves, preferred_element_type=F32).astype(BF16)
    placed = placed.reshape(N_TBL, SLOT_PAD, 2, 128).transpose(0, 2, 1, 3).reshape(N_TBL, 2 * SLOT_PAD, 128)
    got = exchange(
        jnp.concatenate([placed, jnp.broadcast_to(rank_tile[None], (N_TBL, 16, 128))], axis=1), TBL
    )
    rank_zero = from_tiles(got[:, 2 * SLOT_PAD :])
    pooled_slots = (
        got[:, : 2 * SLOT_PAD].reshape(EMB, 2, SLOT_PAD, 128)[:, :, :SLOT_MAX].transpose(2, 0, 1, 3)
    ).reshape(SLOT_MAX * EMB, ROWS)
    pooled = (
        pooled_slots.astype(F32)
        + lax.dot_general(squeeze_own, rank_zero, (((1,), (1,)), ((), ())), preferred_element_type=F32)
    ).astype(BF16)
    partial = jnp.einsum(
        "sbu,seb->sue", incidence.astype(BF16), pooled.reshape(SLOT_MAX, EMB, ROWS), preferred_element_type=F32
    )

    half = SLOT_MAX // 2
    partial = partial.reshape(2, half, 8, 8, 128)
    mine = lax.dynamic_index_in_dim(partial, core, 0, keepdims=False)
    theirs = lax.dynamic_index_in_dim(partial, 1 - core, 0, keepdims=False).astype(BF16)
    swap = [(0, 1), (1, 0)]
    paired = (mine + lax.ppermute(theirs, "core", swap).astype(F32)).astype(BF16)
    got = exchange(paired.transpose(1, 0, 2, 3).reshape(8, half * 8, 128), "z")
    summed = jnp.sum(got.astype(F32), axis=0).astype(BF16)
    got = exchange(jnp.broadcast_to(summed[None], (8, half * 8, 128)), "z")
    here = got.reshape(8, half, 8, 128).transpose(1, 0, 2, 3)
    there = lax.ppermute(here, "core", swap)
    gradient = jnp.where(core == 0, jnp.stack([here, there]), jnp.stack([there, here])).astype(F32)
    gradient = gradient.reshape(SLOT_MAX, TOUCH, EMB)
    history_new = row_accum + jnp.mean(gradient * gradient, axis=2)
    rows_new = table_rows.reshape(SLOT_MAX, TOUCH, EMB) - LEARN_RATE * gradient / (
        jnp.sqrt(history_new)[:, :, None] + EPSILON
    )
    return (rows_new.reshape(SLOT_MAX, TOUCH * EMB), history_new)


def solution(mesh):
    grid = Mesh(mesh.devices.reshape(8, 8, 8, 2), TBL + REP)
    in_specs = (
        P(REP, TBL),
        P(REP, TBL),
        P(REP, None),
        P(REP, None),
        P(None, TBL),
        P(None, TBL),
        P(TBL, None),
        P(TBL, None),
        P(TBL),
        P(TBL),
        P(),
        P(),
        P(TBL, REP, None),
        P(TBL, None),
        P(TBL, None),
    )
    out_specs = (P(TBL, None), P(TBL, None))
    return jax.shard_map(shards, mesh=grid, in_specs=in_specs, out_specs=out_specs, check_vma=False)
```

time: 767 us -> 186 us (0.24)
  blocking collectives: 451 us -> 73.1 us
  waiting for transfers between devices: 264 us -> 60.3 us
    psum x2 -> x0, blocking collectives: 451 us -> none  [rank_sum(): return lax.psum(local_part, 'tbl').astype(jnp.bfloat16)]
    psum x1 -> x0, waiting for transfers between devices: 237 us -> none  [shards(): summed = lax.psum(partial_value, 'rep')]
    all_to_all x0 -> x4, blocking collectives: none -> 73.1 us  [exchange(): return lax.all_to_all(blocks, axis, split_axis=0, concat_axis=0, tiled=True)]
    all_gather x0 -> x1, waiting for transfers between devices: none -> 45.2 us  [shards(): lax.all_gather(squeeze_slots.reshape(SLOT_MAX * 16, 128), REP, axis=0, ti...]
    all_to_all x2, waiting for transfers between devices: 26.2 us -> 13 us  [exchange(): return lax.all_to_all(blocks, axis, split_axis=0, concat_axis=0, tiled=True)]
  transfers between devices with their start and end apart: 3 -> 5, of which waited for: 3 -> 4; matrix products, arithmetic and copies ran while one was open for 1% -> 3% of each run, Pallas kernels for 0% -> 0%
where the time goes in v1:
time: 186 us; the launch traced here: 185 us
  blocking collectives  73.1 us (39%)
  waiting for transfers between devices  60.3 us (32%)
  starting transfers between devices  16.5 us (9%)
  between operations  14.6 us (8%)
  local copies, waits for them, and re-layouts  9.78 us (5%)
  other arithmetic  5.65 us (3%)
  matrix products  4.86 us (3%)
    all_to_all x4, blocking collectives, exchange(): return lax.all_to_all(blocks, axis, split_axis=0, concat_axis=0, tiled=True)  73.1 us
    all_gather x1, waiting for transfers between devices, shards(): lax.all_gather(squeeze_slots.reshape(SLOT_MAX * 16, 128), REP, axis=0, ti...  45.2 us
    all_to_all x2, waiting for transfers between devices, exchange(): return lax.all_to_all(blocks, axis, split_axis=0, concat_axis=0, tiled=True)  13 us
    all_to_all x2, starting transfers between devices, exchange(): return lax.all_to_all(blocks, axis, split_axis=0, concat_axis=0, tiled=True)  9.29 us
    ppermute x1, starting transfers between devices, shards(): there = lax.ppermute(here, 'core', swap)  5.02 us
  transfers between devices with their start and end apart: 5, of which 4 were waited for; matrix products, arithmetic and copies ran while one was open for 3% of the time, Pallas kernels for 0%

profile of v1, /device:TPU:1, one launch (start us, length us, event | category | flops | bytes accessed | tf_op | source)
XLA Modules:
  0.0 184.8 jit_solution(16046418084469366084)
XLA Ops:
  7.2 1.6 convolution_convert_fusion.2
  8.9 0.1 copy.66
  9.1 0.7 constant_dynamic-slice_fusion
  9.8 0.3 convolution_convert_fusion.1
  10.2 0.3 copy.68
  10.6 28.6 %all_to_all.30 = bf16[64,32,128]{2,1,0:T(8,128)(2,1)S(1)} all-to-all(bf16[64,32,128]{2,1,0:T(8,128)(2,1)S(1)} %copy.68), channel_id=1, replica_groups=mesh['y'=8,'x'=8,'z'=8,'core'=2] {'y','x'}, dimensions={0} | all-to-all | bytes 1048576 | tf_op jit(solution)/shard_map/all_to_all | solution.py:27
  39.4 18.4 %all_to_all.31 = bf16[64,16,128]{2,1,0:T(8,128)(2,1)S(1)} all-to-all(bf16[64,16,128]{2,1,0:T(8,128)(2,1)S(1)} %broadcast_in_dim.6), channel_id=1, replica_groups=mesh['y'=8,'x'=8,'z'=8,'core'=2] {'y','x'}, dimensions={0} | all-to-all | bytes 524288 | tf_op jit(solution)/shard_map/all_to_all | solution.py:27
  57.8 0.1 copy.69
  57.9 0.3 convolution_add_fusion.3
  58.3 0.3 convolution_convert_fusion
  58.7 0.2 copy-done.6
  58.9 0.3 fusion.11
  59.2 0.1 copy-done.3
  59.4 0.3 fusion.15
  59.7 0.1 copy.71
  59.9 0.2 copy.88
  60.3 0.8 pad_maximum_fusion.2
  61.2 4.6 %all-to-all-start.2 = ((bf16[64,32,128]{2,1,0:T(8,128)(2,1)}), bf16[64,32,128]{2,1,0:T(8,128)(2,1)S(1)}, u32[]{:S(2)}, u32[]{:S(2)}) async-start(bf16[64,32,128]{2,1,0:T(8,128)(2,1)} %pad_maximum_fusion.2), calls=%async_computation.2 | async-start | bytes 1048576 | tf_op jit(solution)/shard_map/all_to_all | solution.py:27
  65.9 0.1 eq.65
  66.0 0.1 reshape.122
  66.3 0.1 and.27
  66.7 0.2 convolution_convert_fusion.3
  66.8 0.6 copy.79
  67.5 13.0 %all-to-all-done.2 = bf16[64,32,128]{2,1,0:T(8,128)(2,1)S(1)} async-done(((bf16[64,32,128]{2,1,0:T(8,128)(2,1)}), bf16[64,32,128]{2,1,0:T(8,128)(2,1)S(1)}, u32[]{:S(2)}, u32[]{:S(2)}) %all-to-all-start.2) | async-done | bytes 524320 | tf_op jit(solution)/shard_map/all_to_all | solution.py:27
  80.6 0.7 fusion.4
  81.4 1.1 pad_maximum_fusion
  82.6 4.7 %all-to-all-start.3 = ((bf16[64,64,128]{2,1,0:T(8,128)(2,1)}), bf16[64,64,128]{2,1,0:T(8,128)(2,1)S(1)}, u32[]{:S(2)}, u32[]{:S(2)}) async-start(bf16[64,64,128]{2,1,0:T(8,128)(2,1)} %pad_maximum_fusion), calls=%async_computation.3 | async-start | bytes 2097152 | tf_op jit(solution)/shard_map/all_to_all | solution.py:27
  87.2 45.2 %all-gather.2.cloned.1.call-done = bf16[4608,128]{1,0:T(8,128)(2,1)} async-done(((bf16[288,128]{1,0:T(8,128)(2,1)}), bf16[4608,128]{1,0:T(8,128)(2,1)}) %all-gather.2.cloned.1.call-update) | async-done | bytes 1179664 | tf_op jit(solution)/shard_map/all_gather | solution.py:79
  132.4 1.9 %copy.80 = bf16[4,4,18,16,128]{4,1,3,0,2:T(4,128)(2,1)S(1)} copy(bf16[4,4,18,16,128]{4,3,2,1,0:T(8,128)(2,1)} %bitcast.103) | data formatting | bytes 2359296 | tf_op jit(solution)/shard_map/reshape | solution.py:81
  134.5 0.6 copy.75
  135.2 0.1 copy.81
  135.3 0.5 fusion.3
  135.8 1.1 copy-done.1
  137.0 0.3 convolution_bitcast_fusion
  137.3 0.4 copy.82
  137.7 0.2 reshape.143
  137.9 2.2 %collective-permute-start = (bf16[9,8,8,128]{3,2,1,0:T(8,128)(2,1)S(1)}, bf16[9,8,8,128]{3,2,1,0:T(8,128)(2,1)S(1)}, u32[]{:S(2)}, u32[]{:S(2)}) collective-permute-start(bf16[9,8,8,128]{3,2,1,0:T(8,128)(2,1)S(1)} %fusion.28), channel_id=1, source_target_pairs={{0,1},{1,0},{2,3},{3,2},{4,5},{5,4},{6,7},{7,6},{8,9},{9,8},{10,11... | collective-permute-start | bytes 442376 | tf_op jit(solution)/shard_map/ppermute | solution.py:125
  140.1 1.1 collective-permute-done
  141.2 15.5 %all_to_all.32 = bf16[8,72,128]{2,1,0:T(8,128)(2,1)S(1)} all-to-all(bf16[8,72,128]{2,1,0:T(8,128)(2,1)S(1)} %copy_bitcast_fusion), channel_id=1, replica_groups=mesh['y'=8,'x'=8,'z'=8,'core'=2] {'z'}, dimensions={0} | all-to-all | bytes 294912 | tf_op jit(solution)/shard_map/all_to_all | solution.py:27
  156.8 10.6 %all_to_all.33 = bf16[8,72,128]{2,1,0:T(8,128)(2,1)S(1)} all-to-all(bf16[8,72,128]{2,1,0:T(8,128)(2,1)S(1)} %broadcast_in_dim.8), channel_id=1, replica_groups=mesh['y'=8,'x'=8,'z'=8,'core'=2] {'z'}, dimensions={0} | all-to-all | bytes 294912 | tf_op jit(solution)/shard_map/all_to_all | solution.py:27
  167.3 5.0 %collective-permute-start.1 = (bf16[9,8,8,128]{3,2,0,1:T(8,128)(2,1)S(1)}, bf16[9,8,8,128]{3,2,0,1:T(8,128)(2,1)S(1)}, u32[]{:S(2)}, u32[]{:S(2)}) collective-permute-start(bf16[9,8,8,128]{3,2,0,1:T(8,128)(2,1)S(1)} %bitcast.113), channel_id=1, source_target_pairs={{0,1},{1,0},{2,3},{3,2},{4,5},{5,4},{6,7},{7,6},{8,9},{9,8},{10,11... | collective-permute-start | bytes 442376 | tf_op jit(solution)/shard_map/ppermute | solution.py:130
  172.4 1.0 collective-permute-done.1
  173.5 0.2 mul.64
  173.8 0.4 reduce_sum.48
  174.2 0.6 sqrt_add_fusion
  174.8 0.4 div.30
  175.2 0.4 div.31
  175.8 2.1 %divide_subtract_fusion = f32[18,8192]{1,0:T(8,128)} fusion(f32[18,8192]{1,0:T(8,128)} %param.28, f32[18,8192]{1,0:T(8,128)S(1)} %mul.62, f32[18,8192]{1,0:T(8,128)S(1)} %div.31), kind=kLoop, calls=%fused_computation.25 | loop fusion | flops 294912 | bytes 2359296 | tf_op jit(solution)/shard_map/sub | solution.py:134
  (56 shorter events, 2.0 us)
Async XLA Ops:
  7.2 51.1 %copy-start = (bf16[512,384]{1,0:T(8,128)(2,1)S(1)}, bf16[512,384]{1,0:T(8,128)(2,1)}, u32[]{:S(2)}) copy-start(bf16[512,384]{1,0:T(8,128)(2,1)} %param.19) | copy-start | bytes 1179652
  7.2 1.8 copy-start.10
  39.2 18.7 %copy-start.2 = (bf16[256,384]{1,0:T(8,128)(2,1)S(1)}, bf16[256,384]{1,0:T(8,128)(2,1)}, u32[]{:S(2)}) copy-start(bf16[256,384]{1,0:T(8,128)(2,1)} %param.16) | copy-start | bytes 589828
  39.2 18.7 %copy-start.5 = (bf16[384,512]{1,0:T(8,128)(2,1)S(1)}, bf16[384,512]{1,0:T(8,128)(2,1)}, u32[]{:S(2)}) copy-start(bf16[384,512]{1,0:T(8,128)(2,1)} %param.22) | copy-start | bytes 1179652
  39.4 18.9 %copy-start.4 = (bf16[256,384]{1,0:T(8,128)(2,1)S(1)}, bf16[256,384]{1,0:T(8,128)(2,1)}, u32[]{:S(2)}) copy-start(bf16[256,384]{1,0:T(8,128)(2,1)} %param.15) | copy-start | bytes 589828
  57.9 1.0 copy-start.6
  57.9 0.9 copy-start.11
  58.3 1.0 copy-start.3
  58.3 1.1 copy-start.7
  58.3 1.1 copy-start.12
  60.3 5.5 %copy-start.9 = (s32[384]{0:T(512)S(1)}, s32[384]{0:T(512)}, u32[]{:S(2)}) copy-start(s32[384]{0:T(512)} %param.26) | copy-start | bytes 4612
  61.2 19.3 %all-to-all-start.2 = ((bf16[64,32,128]{2,1,0:T(8,128)(2,1)}), bf16[64,32,128]{2,1,0:T(8,128)(2,1)S(1)}, u32[]{:S(2)}, u32[]{:S(2)}) async-start(bf16[64,32,128]{2,1,0:T(8,128)(2,1)} %pad_maximum_fusion.2), calls=%async_computation.2 | async-start | bytes 1048576 | tf_op jit(solution)/shard_map/all_to_all | solution.py:27
  65.8 66.6 %all-gather.2.cloned.1.call-start = ((), (), s32[]{:S(2)}) async-start(), calls=%async_computation.6 | async-start | bytes 1253376 | tf_op jit(solution)/shard_map/all_gather | solution.py:79
  82.6 51.7 %all-to-all-start.3 = ((bf16[64,64,128]{2,1,0:T(8,128)(2,1)}), bf16[64,64,128]{2,1,0:T(8,128)(2,1)S(1)}, u32[]{:S(2)}, u32[]{:S(2)}) async-start(bf16[64,64,128]{2,1,0:T(8,128)(2,1)} %pad_maximum_fusion), calls=%async_computation.3 | async-start | bytes 2097152 | tf_op jit(solution)/shard_map/all_to_all | solution.py:27
  135.3 1.7 copy-start.1
  137.9 3.3 %collective-permute-start = (bf16[9,8,8,128]{3,2,1,0:T(8,128)(2,1)S(1)}, bf16[9,8,8,128]{3,2,1,0:T(8,128)(2,1)S(1)}, u32[]{:S(2)}, u32[]{:S(2)}) collective-permute-start(bf16[9,8,8,128]{3,2,1,0:T(8,128)(2,1)S(1)} %fusion.28), channel_id=1, source_target_pairs={{0,1},{1,0},{2,3},{3,2},{4,5},{5,4},{6,7},{7,6},{8,9},{9,8},{10,11... | collective-permute-start | bytes 442376 | tf_op jit(solution)/shard_map/ppermute | solution.py:125
  167.3 6.0 %collective-permute-start.1 = (bf16[9,8,8,128]{3,2,0,1:T(8,128)(2,1)S(1)}, bf16[9,8,8,128]{3,2,0,1:T(8,128)(2,1)S(1)}, u32[]{:S(2)}, u32[]{:S(2)}) collective-permute-start(bf16[9,8,8,128]{3,2,0,1:T(8,128)(2,1)S(1)} %bitcast.113), channel_id=1, source_target_pairs={{0,1},{1,0},{2,3},{3,2},{4,5},{5,4},{6,7},{7,6},{8,9},{9,8},{10,11... | collective-permute-start | bytes 442376 | tf_op jit(solution)/shard_map/ppermute | solution.py:130
  173.5 0.7 copy-start.8
Sparse Core Ops, SparseCore 0:
  69.4 63.0 all-gather.1

commit v2 on v1

v2 whole, which is shorter than its diff:
```python
import jax
import jax.numpy as jnp
from jax import lax
from jax.sharding import Mesh, PartitionSpec as P

FEATS = 384
EMB = 64
RANK = 512
ROWS = 256
TOUCH = 128
SLOT_MAX = 18
N_TBL = 64
N_REP = 16
PER_DEV = FEATS // N_TBL

LEARN_RATE = 0.25
EPSILON = 1e-06

TBL = ("y", "x")
REP = ("z", "core")
BF16 = jnp.bfloat16
F32 = jnp.float32


def exchange(blocks, axis):
    return lax.all_to_all(blocks, axis, split_axis=0, concat_axis=0, tiled=True)


def to_tiles(matrix):
    return matrix.reshape(16, 16, 4, 128).transpose(0, 2, 1, 3).reshape(64, 16, 128)


def from_tiles(tiles):
    return tiles.reshape(16, 4, 16, 128).transpose(0, 2, 1, 3).reshape(ROWS, RANK)


def shards(
    x_zero,
    grad_top,
    low_zero,
    low_one,
    lift_zero,
    lift_one,
    squeeze_zero,
    squeeze_one,
    bias_zero,
    bias_one,
    table_owner,
    table_slot,
    incidence,
    table_rows,
    row_accum,
):
    rep = lax.axis_index(REP)
    core = lax.axis_index("core")
    odd = lax.axis_index("z") % 2
    upstream = grad_top.astype(F32)
    embedded = x_zero.astype(F32)

    place = table_owner * SLOT_MAX + table_slot
    wanted = (jnp.arange(N_TBL * SLOT_MAX)[:, None] == place[None, :]).astype(BF16)

    part_one = lax.dot_general(
        (upstream * embedded).astype(BF16), lift_one, (((1,), (1,)), ((), ())), preferred_element_type=F32
    ).astype(BF16)
    quarter = lax.dynamic_slice(squeeze_zero, (0, (2 * odd + core) * 128), (PER_DEV * EMB, 128))
    quarter = quarter.reshape(PER_DEV, EMB, 128).transpose(1, 0, 2)
    got = exchange(jnp.concatenate([to_tiles(part_one), quarter], axis=1), TBL)
    rank_tile = jnp.sum(got[:, :16].astype(F32), axis=0).astype(BF16)
    quarter = jnp.dot(wanted, got[:, 16:].reshape(FEATS, 128), preferred_element_type=F32).astype(BF16)
    got = exchange(
        jnp.concatenate(
            [jnp.broadcast_to(rank_tile[None], (N_TBL, 16, 128)), quarter.reshape(N_TBL, SLOT_MAX, 128)], axis=1
        ),
        TBL,
    )
    rank_one = from_tiles(got[:, :16])

    quarter = got[:, 16:].transpose(1, 0, 2)
    other = lax.ppermute(quarter, "core", [(0, 1), (1, 0)])
    part = jnp.where(core == 0, jnp.concatenate([quarter, other], axis=2), jnp.concatenate([other, quarter], axis=2))
    other = lax.ppermute(part, "z", [(i, i ^ 1) for i in range(8)])
    squeeze_own = jnp.where(odd == 0, jnp.concatenate([part, other], axis=2), jnp.concatenate([other, part], axis=2))

    gate_one = jnp.dot(low_one, lift_one, preferred_element_type=F32) + bias_one
    gate_zero = jnp.dot(low_zero, lift_zero, preferred_element_type=F32) + bias_zero
    grad_mid = upstream + lax.dot_general(
        rank_one, squeeze_one, (((1,), (1,)), ((), ())), preferred_element_type=F32
    )
    part_zero = lax.dot_general(
        (grad_mid * embedded).astype(BF16), lift_zero, (((1,), (1,)), ((), ())), preferred_element_type=F32
    ).astype(BF16)
    pooled_local = (upstream * gate_one + grad_mid * gate_zero + grad_mid).astype(BF16)
    by_column = pooled_local.reshape(2, 128, PER_DEV, EMB).transpose(3, 0, 2, 1).reshape(N_TBL, 2 * PER_DEV, 128)
    got = exchange(jnp.concatenate([to_tiles(part_zero), by_column], axis=1), TBL)
    rank_tile = jnp.sum(got[:, :16].astype(F32), axis=0).astype(BF16)

    placed = [
        jnp.dot(
            wanted,
            got[:, 16 + h * PER_DEV : 16 + (h + 1) * PER_DEV].reshape(FEATS, 128),
            preferred_element_type=F32,
        )
        .astype(BF16)
        .reshape(N_TBL, SLOT_MAX, 128)
        for h in range(2)
    ]
    got = exchange(jnp.concatenate([jnp.broadcast_to(rank_tile[None], (N_TBL, 16, 128))] + placed, axis=1), TBL)
    rank_zero = from_tiles(got[:, :16])
    pooled_slots = (
        got[:, 16:].reshape(EMB, 2, SLOT_MAX, 128).transpose(2, 0, 1, 3).reshape(SLOT_MAX * EMB, ROWS)
    )
    pooled = (
        pooled_slots.astype(F32)
        + lax.dot_general(
            squeeze_own.reshape(SLOT_MAX * EMB, RANK),
            rank_zero,
            (((1,), (1,)), ((), ())),
            preferred_element_type=F32,
        )
    ).astype(BF16)
    partial = jnp.einsum(
        "sbu,seb->sue", incidence.astype(BF16), pooled.reshape(SLOT_MAX, EMB, ROWS), preferred_element_type=F32
    ).astype(BF16)

    share = TOUCH // N_REP
    got = exchange(partial.reshape(SLOT_MAX, N_REP, 4, 128).transpose(1, 0, 2, 3).reshape(N_REP, SLOT_MAX * 4, 128), REP)
    gradient = jnp.sum(got.astype(F32), axis=0).reshape(SLOT_MAX, 4, 2, EMB)
    history = lax.dynamic_slice(row_accum, (0, rep * share), (SLOT_MAX, share)).reshape(SLOT_MAX, 4, 2)
    history_new = history + jnp.mean(gradient * gradient, axis=3)
    update = LEARN_RATE * gradient / (jnp.sqrt(history_new)[:, :, :, None] + EPSILON)
    update = update.astype(BF16).reshape(SLOT_MAX * 4, 128)
    terms, rest = [], history_new.reshape(SLOT_MAX * share)
    for _ in range(3):
        term = lax.reduce_precision(rest, 8, 7)
        terms.append(term)
        rest = rest - term
    terms = jnp.pad(jnp.concatenate(terms).astype(BF16), (0, 8 * 128 - 3 * SLOT_MAX * share)).reshape(8, 128)
    send = jnp.concatenate([update, terms], axis=0)
    got = exchange(jnp.broadcast_to(send[None], (N_REP,) + send.shape), REP)
    update = got[:, : SLOT_MAX * 4].reshape(N_REP, SLOT_MAX, 4 * 128).transpose(1, 0, 2).reshape(SLOT_MAX, TOUCH * EMB)
    terms = got[:, SLOT_MAX * 4 :].reshape(N_REP, 8 * 128)[:, : 3 * SLOT_MAX * share].astype(F32)
    terms = terms.reshape(N_REP, 3, SLOT_MAX, share)
    history_new = (terms[:, 2] + terms[:, 1]) + terms[:, 0]
    history_new = history_new.transpose(1, 0, 2).reshape(SLOT_MAX, TOUCH)
    return (table_rows - update.astype(F32), history_new)


def solution(mesh):
    grid = Mesh(mesh.devices.reshape(8, 8, 8, 2), TBL + REP)
    in_specs = (
        P(REP, TBL),
        P(REP, TBL),
        P(REP, None),
        P(REP, None),
        P(None, TBL),
        P(None, TBL),
        P(TBL, None),
        P(TBL, None),
        P(TBL),
        P(TBL),
        P(),
        P(),
        P(TBL, REP, None),
        P(TBL, None),
        P(TBL, None),
    )
    out_specs = (P(TBL, None), P(TBL, None))
    return jax.shard_map(shards, mesh=grid, in_specs=in_specs, out_specs=out_specs, check_vma=False)
```

time: 186 us -> 178 us (0.957)
  starting transfers between devices: 16.5 us -> 61.4 us
  waiting for transfers between devices: 60.3 us -> 38.4 us
  blocking collectives: 73.1 us -> 56.4 us
  between operations: 14.6 us -> 1.33 us
    all_gather x1 -> x0, waiting for transfers between devices: 45.2 us -> none  [shards(): lax.all_gather(squeeze_slots.reshape(SLOT_MAX * 16, 128), REP, axis=0, ti...]
    all_to_all x2 -> x3, starting transfers between devices: 9.29 us -> 40.6 us  [exchange(): return lax.all_to_all(blocks, axis, split_axis=0, concat_axis=0, tiled=True)]
    all_to_all x4 -> x3, blocking collectives: 73.1 us -> 56.4 us  [exchange(): return lax.all_to_all(blocks, axis, split_axis=0, concat_axis=0, tiled=True)]
    ppermute x2, starting transfers between devices: 7.18 us -> 20.8 us  [the longest x1 11.1 us: shards(): other = lax.ppermute(part, 'z', [(i, i ^ 1) for i in range(8)])]
    all_to_all x2 -> x3, waiting for transfers between devices: 13 us -> 25.7 us  [exchange(): return lax.all_to_all(blocks, axis, split_axis=0, concat_axis=0, tiled=True)]
    ppermute x2, waiting for transfers between devices: 2.08 us -> 12.8 us  [the longest x1 11.4 us: shards(): other = lax.ppermute(part, 'z', [(i, i ^ 1) for i in range(8)])]
  transfers between devices with their start and end apart: 5 -> 5, of which waited for: 4 -> 4; matrix products, arithmetic and copies ran while one was open for 3% -> 1% of each run, Pallas kernels for 0% -> 0%
where the time goes in v2:
time: 178 us; the launch traced here: 177 us
  starting transfers between devices  61.4 us (34%)
  blocking collectives  56.4 us (32%)
  waiting for transfers between devices  38.4 us (22%)
  local copies, waits for them, and re-layouts  10.4 us (6%)
  matrix products  4.98 us (3%)
  other arithmetic  4.21 us (2%)
    all_to_all x3, blocking collectives, exchange(): return lax.all_to_all(blocks, axis, split_axis=0, concat_axis=0, tiled=True)  56.4 us
    all_to_all x3, starting transfers between devices, exchange(): return lax.all_to_all(blocks, axis, split_axis=0, concat_axis=0, tiled=True)  40.6 us
    all_to_all x3, waiting for transfers between devices, exchange(): return lax.all_to_all(blocks, axis, split_axis=0, concat_axis=0, tiled=True)  25.7 us
    ppermute x1, waiting for transfers between devices, shards(): other = lax.ppermute(part, 'z', [(i, i ^ 1) for i in range(8)])  11.4 us
    ppermute x1, starting transfers between devices, shards(): other = lax.ppermute(part, 'z', [(i, i ^ 1) for i in range(8)])  11.1 us
    ppermute x1, starting transfers between devices, shards(): other = lax.ppermute(quarter, 'core', [(0, 1), (1, 0)])  9.7 us
  transfers between devices with their start and end apart: 5, of which 4 were waited for; matrix products, arithmetic and copies ran while one was open for 1% of the time, Pallas kernels for 0%

profile of v2, /device:TPU:1, one launch (start us, length us, event | category | flops | bytes accessed | tf_op | source)
XLA Modules:
  0.0 177.1 jit_solution(3284521677177521570)
XLA Ops:
  0.7 0.9 constant_dynamic-slice_fusion.1
  1.7 1.5 convolution_convert_fusion.5
  3.4 0.8 pad_maximum_fusion.3
  4.2 14.0 %all-to-all-start = ((bf16[64,22,128]{2,1,0:T(8,128)(2,1)}), bf16[64,22,128]{2,1,0:T(8,128)(2,1)S(1)}, u32[]{:S(2)}, u32[]{:S(2)}) async-start(bf16[64,22,128]{2,1,0:T(8,128)(2,1)} %pad_maximum_fusion.3), calls=%async_computation | async-start | bytes 786432 | tf_op jit(solution)/shard_map/all_to_all | solution.py:26
  18.2 13.5 %all-to-all-done = bf16[64,22,128]{2,1,0:T(8,128)(2,1)S(1)} async-done(((bf16[64,22,128]{2,1,0:T(8,128)(2,1)}), bf16[64,22,128]{2,1,0:T(8,128)(2,1)S(1)}, u32[]{:S(2)}, u32[]{:S(2)}) %all-to-all-start) | async-done | bytes 360480 | tf_op jit(solution)/shard_map/all_to_all | solution.py:26
  31.9 0.4 convolution_convert_fusion.2
  32.6 20.4 %all_to_all.30 = bf16[64,34,128]{2,1,0:T(8,128)(2,1)S(1)} all-to-all(bf16[64,34,128]{2,1,0:T(8,128)(2,1)S(1)} %pad_maximum_fusion.1), channel_id=1, replica_groups=mesh['y'=8,'x'=8,'z'=8,'core'=2] {'y','x'}, dimensions={0} | all-to-all | bytes 1114112 | tf_op jit(solution)/shard_map/all_to_all | solution.py:26
  53.2 0.3 convolution_add_fusion.3
  53.6 0.3 convolution_convert_fusion.4
  54.1 0.3 fusion.4
  54.4 0.1 copy-done.3
  54.7 0.3 fusion.12
  55.0 0.1 copy.117
  55.2 0.1 copy.119
  55.4 20.2 %all_to_all.31 = bf16[64,28,128]{2,1,0:T(8,128)(2,1)S(1)} all-to-all(bf16[64,28,128]{2,1,0:T(8,128)(2,1)S(1)} %pad_maximum_fusion.2), channel_id=1, replica_groups=mesh['y'=8,'x'=8,'z'=8,'core'=2] {'y','x'}, dimensions={0} | all-to-all | bytes 917504 | tf_op jit(solution)/shard_map/all_to_all | solution.py:26
  75.8 0.4 convolution_convert_fusion
  76.4 0.4 convolution_convert_fusion.1
  77.0 1.1 pad_maximum_fusion
  78.1 4.8 %all-to-all-start.3 = ((bf16[64,52,128]{2,1,0:T(8,128)(2,1)}), bf16[64,52,128]{2,1,0:T(8,128)(2,1)S(1)}, u32[]{:S(2)}, u32[]{:S(2)}) async-start(bf16[64,52,128]{2,1,0:T(8,128)(2,1)} %pad_maximum_fusion), calls=%async_computation.3 | async-start | bytes 1835008 | tf_op jit(solution)/shard_map/all_to_all | solution.py:26
  83.0 9.7 %collective-permute-start = (bf16[18,64,128]{2,0,1:T(8,128)(2,1)S(1)}, bf16[18,64,128]{2,0,1:T(8,128)(2,1)S(1)}, u32[]{:S(2)}, u32[]{:S(2)}) collective-permute-start(bf16[18,64,128]{2,0,1:T(8,128)(2,1)S(1)} %slice_bitcast_fusion), channel_id=1, source_target_pairs={{0,1},{1,0},{2,3},{3,2},{4,5},{5,4},{6,7},{7,6},{8,9},{9,8},{10,11... | collective-permute-start | bytes 884744 | tf_op jit(solution)/shard_map/ppermute | solution.py:80
  92.7 1.3 collective-permute-done
  94.0 0.3 maximum_select_fusion.2
  94.3 0.1 copy.124
  94.4 11.1 %collective-permute-start.1 = (bf16[18,64,256]{2,1,0:T(8,128)(2,1)S(1)}, bf16[18,64,256]{2,1,0:T(8,128)(2,1)S(1)}, u32[]{:S(2)}, u32[]{:S(2)}) collective-permute-start(bf16[18,64,256]{2,1,0:T(8,128)(2,1)S(1)} %copy.124), channel_id=1, source_target_pairs={{0,2},{2,0},{4,6},{6,4},{8,10},{10,8},{12,14},{14,12},{1,3},{3,1},... | collective-permute-start | bytes 1769480 | tf_op jit(solution)/shard_map/ppermute | solution.py:82
  105.6 0.2 maximum_select_fusion.3
  105.9 0.1 copy.139
  106.2 0.1 convert_bitcast_fusion
  106.3 0.9 copy.121
  107.3 11.4 %collective-permute-done.1 = bf16[18,64,256]{2,1,0:T(8,128)(2,1)S(1)} collective-permute-done((bf16[18,64,256]{2,1,0:T(8,128)(2,1)S(1)}, bf16[18,64,256]{2,1,0:T(8,128)(2,1)S(1)}, u32[]{:S(2)}, u32[]{:S(2)}) %collective-permute-start.1) | collective-permute-done | bytes 589856 | tf_op jit(solution)/shard_map/ppermute | solution.py:82
  118.7 0.5 fusion
  119.2 1.1 copy-done.1
  120.4 0.3 fusion.13
  120.7 0.3 copy.126
  121.1 0.3 reshape.151
  121.4 0.8 copy.128
  122.2 21.8 %all-to-all-start.4 = ((bf16[16,72,128]{2,1,0:T(8,128)(2,1)}), bf16[16,72,128]{2,1,0:T(8,128)(2,1)S(1)}, u32[]{:S(2)}, u32[]{:S(2)}) async-start(bf16[16,72,128]{2,1,0:T(8,128)(2,1)} %copy.128), calls=%async_computation.4 | async-start | bytes 589824 | tf_op jit(solution)/shard_map/all_to_all | solution.py:26
  144.3 12.1 %all-to-all-done.4 = bf16[16,72,128]{2,1,0:T(8,128)(2,1)S(1)} async-done(((bf16[16,72,128]{2,1,0:T(8,128)(2,1)}), bf16[16,72,128]{2,1,0:T(8,128)(2,1)S(1)}, u32[]{:S(2)}, u32[]{:S(2)}) %all-to-all-start.4) | async-done | bytes 294944 | tf_op jit(solution)/shard_map/all_to_all | solution.py:26
  156.5 0.2 reduce_sum.45
  157.0 0.1 div.21
  157.4 0.1 div.24
  157.7 15.8 %all_to_all.32 = bf16[16,80,128]{2,1,0:T(8,128)(2,1)S(1)} all-to-all(bf16[16,80,128]{2,1,0:T(8,128)(2,1)S(1)} %broadcast_in_dim.8), channel_id=1, replica_groups=mesh['y'=8,'x'=8,'z'=8,'core'=2] {'z','core'}, dimensions={0} | all-to-all | bytes 655360 | tf_op jit(solution)/shard_map/all_to_all | solution.py:26
  173.5 0.2 copy.136
  173.7 0.1 copy.137
  173.9 0.7 copy.138
  174.7 0.3 copy.135
  175.1 0.5 copy.144
  175.6 0.6 copy-done.5
  176.2 1.0 sub.11
  (80 shorter events, 3.2 us)
Async XLA Ops:
  0.6 52.9 %copy-start = (bf16[512,384]{1,0:T(8,128)(2,1)S(1)}, bf16[512,384]{1,0:T(8,128)(2,1)}, u32[]{:S(2)}) copy-start(bf16[512,384]{1,0:T(8,128)(2,1)} %param.19) | copy-start | bytes 1179652
  3.2 15.0 %copy-start.11 = (s32[384]{0:T(512)S(1)}, s32[384]{0:T(512)}, u32[]{:S(2)}) copy-start(s32[384]{0:T(512)} %param.26) | copy-start | bytes 4612
  3.2 15.0 %copy-start.12 = (s32[384]{0:T(512)S(1)}, s32[384]{0:T(512)}, u32[]{:S(2)}) copy-start(s32[384]{0:T(512)} %param.25) | copy-start | bytes 4612
  4.2 27.6 %all-to-all-start = ((bf16[64,22,128]{2,1,0:T(8,128)(2,1)}), bf16[64,22,128]{2,1,0:T(8,128)(2,1)S(1)}, u32[]{:S(2)}, u32[]{:S(2)}) async-start(bf16[64,22,128]{2,1,0:T(8,128)(2,1)} %pad_maximum_fusion.3), calls=%async_computation | async-start | bytes 786432 | tf_op jit(solution)/shard_map/all_to_all | solution.py:26
  32.5 20.7 %copy-start.2 = (bf16[256,384]{1,0:T(8,128)(2,1)S(1)}, bf16[256,384]{1,0:T(8,128)(2,1)}, u32[]{:S(2)}) copy-start(bf16[256,384]{1,0:T(8,128)(2,1)} %param.16) | copy-start | bytes 589828
  32.5 20.7 %copy-start.6 = (bf16[384,512]{1,0:T(8,128)(2,1)S(1)}, bf16[384,512]{1,0:T(8,128)(2,1)}, u32[]{:S(2)}) copy-start(bf16[384,512]{1,0:T(8,128)(2,1)} %param.22) | copy-start | bytes 1179652
  32.6 20.9 %copy-start.4 = (bf16[256,384]{1,0:T(8,128)(2,1)S(1)}, bf16[256,384]{1,0:T(8,128)(2,1)}, u32[]{:S(2)}) copy-start(bf16[256,384]{1,0:T(8,128)(2,1)} %param.15) | copy-start | bytes 589828
  53.2 1.0 copy-start.7
  53.2 0.9 copy-start.10
  53.6 1.0 copy-start.3
  53.6 1.1 copy-start.8
  53.6 1.1 copy-start.13
  78.1 27.7 %all-to-all-start.3 = ((bf16[64,52,128]{2,1,0:T(8,128)(2,1)}), bf16[64,52,128]{2,1,0:T(8,128)(2,1)S(1)}, u32[]{:S(2)}, u32[]{:S(2)}) async-start(bf16[64,52,128]{2,1,0:T(8,128)(2,1)} %pad_maximum_fusion), calls=%async_computation.3 | async-start | bytes 1835008 | tf_op jit(solution)/shard_map/all_to_all | solution.py:26
  83.0 11.0 %collective-permute-start = (bf16[18,64,128]{2,0,1:T(8,128)(2,1)S(1)}, bf16[18,64,128]{2,0,1:T(8,128)(2,1)S(1)}, u32[]{:S(2)}, u32[]{:S(2)}) collective-permute-start(bf16[18,64,128]{2,0,1:T(8,128)(2,1)S(1)} %slice_bitcast_fusion), channel_id=1, source_target_pairs={{0,1},{1,0},{2,3},{3,2},{4,5},{5,4},{6,7},{7,6},{8,9},{9,8},{10,11... | collective-permute-start | bytes 884744 | tf_op jit(solution)/shard_map/ppermute | solution.py:80
  94.4 24.3 %collective-permute-start.1 = (bf16[18,64,256]{2,1,0:T(8,128)(2,1)S(1)}, bf16[18,64,256]{2,1,0:T(8,128)(2,1)S(1)}, u32[]{:S(2)}, u32[]{:S(2)}) collective-permute-start(bf16[18,64,256]{2,1,0:T(8,128)(2,1)S(1)} %copy.124), channel_id=1, source_target_pairs={{0,2},{2,0},{4,6},{6,4},{8,10},{10,8},{12,14},{14,12},{1,3},{3,1},... | collective-permute-start | bytes 1769480 | tf_op jit(solution)/shard_map/ppermute | solution.py:82
  118.7 1.7 copy-start.1
  120.7 23.3 %copy-start.9 = (f32[18,128]{1,0:T(8,128)S(1)}, f32[18,128]{1,0:T(8,128)}, u32[]{:S(2)}) copy-start(f32[18,128]{1,0:T(8,128)} %param.29) | copy-start | bytes 27652
  122.2 34.2 %all-to-all-start.4 = ((bf16[16,72,128]{2,1,0:T(8,128)(2,1)}), bf16[16,72,128]{2,1,0:T(8,128)(2,1)S(1)}, u32[]{:S(2)}, u32[]{:S(2)}) async-start(bf16[16,72,128]{2,1,0:T(8,128)(2,1)} %copy.128), calls=%async_computation.4 | async-start | bytes 589824 | tf_op jit(solution)/shard_map/all_to_all | solution.py:26
  175.0 1.1 copy-start.5

commit v3 on v2

v3 whole, which is shorter than its diff:
```python
import jax
import jax.numpy as jnp
from jax import lax
from jax.experimental import pallas as pl
from jax.experimental.pallas import tpu as pltpu
from jax.sharding import Mesh, PartitionSpec as P

FEATS = 384
EMB = 64
RANK = 512
ROWS = 256
TOUCH = 128
SLOT_MAX = 18
N_TBL = 64
N_REP = 16
PER_DEV = FEATS // N_TBL
SLOT_ROWS = SLOT_MAX // 2
UPDATE_ROWS = SLOT_MAX * 4
SEND_ROWS = UPDATE_ROWS + 8

LEARN_RATE = 0.25
EPSILON = 1e-06

TBL = ("y", "x")
REP = ("z", "core")
BF16 = jnp.bfloat16
F32 = jnp.float32


def exchange(blocks, axis):
    return lax.all_to_all(blocks, axis, split_axis=0, concat_axis=0, tiled=True)


def to_tiles(matrix):
    return matrix.reshape(16, 16, 4, 128).transpose(0, 2, 1, 3).reshape(64, 16, 128)


def from_tiles(tiles):
    return tiles.reshape(16, 4, 16, 128).transpose(0, 2, 1, 3).reshape(ROWS, RANK)


def first_kernel(x_hbm, top_hbm, lift_hbm, squeeze_hbm, out_ref, x_ref, top_ref, lift_ref, squeeze_ref, sems):
    height, core = lax.axis_index("z"), lax.axis_index("core")
    quarter = pl.multiple_of((2 * (height % 2) + core) * 128, 128)
    copies = []
    for source, target, pieces in (
        (x_hbm, x_ref, 2),
        (top_hbm, top_ref, 2),
        (lift_hbm, lift_ref, 4),
        (squeeze_hbm.at[:, pl.ds(quarter, 128)], squeeze_ref, 2),
    ):
        rows = target.shape[0] // pieces
        for i in range(pieces):
            part = pl.ds(i * rows, rows)
            copies.append(pltpu.make_async_copy(source.at[part], target.at[part], sems.at[len(copies)]))
    for copy in copies:
        copy.start()
    row = lax.broadcasted_iota(jnp.int32, (N_TBL * 8, FEATS), 0)
    col = lax.broadcasted_iota(jnp.int32, (N_TBL * 8, FEATS), 1)
    table, column = row & 7, (row >> 4) + 32 * ((height // 2) % 2)
    pick = jnp.where((col == table * EMB + column) & (table < PER_DEV), 1.0, 0.0).astype(BF16)
    for copy in copies:
        copy.wait()
    scaled = (top_ref[...].astype(F32) * x_ref[...].astype(F32)).astype(BF16)
    part = lax.dot_general(scaled, lift_ref[...], (((1,), (1,)), ((), ())), preferred_element_type=F32).astype(BF16)
    for i in range(16):
        for j in range(4):
            out_ref[4 * i + j, :16, :] = part[16 * i : 16 * i + 16, 128 * j : 128 * j + 128]
    moved = jnp.dot(pick, squeeze_ref[...], preferred_element_type=F32)
    out_ref[:, 16:, :] = moved.reshape(N_TBL, 8, 128).astype(BF16)


def first_step(x_zero, grad_top, lift_one, squeeze_zero):
    return pl.pallas_call(
        first_kernel,
        out_shape=jax.ShapeDtypeStruct((N_TBL, 24, 128), BF16),
        in_specs=[pl.BlockSpec(memory_space=pl.ANY)] * 4,
        out_specs=pl.BlockSpec(memory_space=pltpu.VMEM),
        scratch_shapes=[
            pltpu.VMEM(x_zero.shape, BF16),
            pltpu.VMEM(grad_top.shape, BF16),
            pltpu.VMEM(lift_one.shape, BF16),
            pltpu.VMEM((PER_DEV * EMB, 128), BF16),
            pltpu.SemaphoreType.DMA((10,)),
        ],
        compiler_params=pltpu.CompilerParams(vmem_limit_bytes=60 * 2**20),
        name="first_step",
    )(x_zero, grad_top, lift_one, squeeze_zero)


def last_kernel(got_ref, rows_ref, rows_out, history_out, wide):
    wide[...] = got_ref[...].astype(F32).reshape(N_REP * SEND_ROWS, 128)
    for i in range(EMB):
        first = (i // 4) * SEND_ROWS + i % 4
        update = wide[pl.ds(first, SLOT_MAX, stride=4), :]
        rows_out[:, 128 * i : 128 * i + 128] = rows_ref[:, 128 * i : 128 * i + 128] - update
    terms = jnp.concatenate(
        [wide[j * SEND_ROWS + UPDATE_ROWS : (j + 1) * SEND_ROWS, :] for j in range(N_REP)], axis=0
    ).T
    history_out[...] = (terms[64 : 64 + SLOT_MAX] + terms[32 : 32 + SLOT_MAX]) + terms[:SLOT_MAX]


def last_step(got, table_rows):
    vmem = pl.BlockSpec(memory_space=pltpu.VMEM)
    return pl.pallas_call(
        last_kernel,
        out_shape=(
            jax.ShapeDtypeStruct((SLOT_MAX, TOUCH * EMB), F32),
            jax.ShapeDtypeStruct((SLOT_MAX, TOUCH), F32),
        ),
        in_specs=[vmem, vmem],
        out_specs=(vmem, vmem),
        scratch_shapes=[pltpu.VMEM((N_REP * SEND_ROWS, 128), F32)],
        compiler_params=pltpu.CompilerParams(vmem_limit_bytes=24 * 2**20),
        name="last_step",
    )(got, table_rows)


def both(mine, other, bit, axis):
    return jnp.where(bit == 0, jnp.concatenate([mine, other], axis), jnp.concatenate([other, mine], axis))


def shards(
    x_zero,
    grad_top,
    low_zero,
    low_one,
    lift_zero,
    lift_one,
    squeeze_zero,
    squeeze_one,
    bias_zero,
    bias_one,
    table_owner,
    table_slot,
    incidence,
    table_rows,
    row_accum,
):
    rep = lax.axis_index(REP)
    core = lax.axis_index("core")
    height = lax.axis_index("z")
    half, quarter = (height // 2) % 2, rep % 4
    upstream = grad_top.astype(F32)
    embedded = x_zero.astype(F32)

    place = table_owner * SLOT_MAX + table_slot
    wanted = (jnp.arange(N_TBL * SLOT_MAX)[:, None] == place[None, :]).astype(BF16)
    later = 2 * jnp.arange(SLOT_ROWS) + lax.axis_index(TBL) % 2
    second = (jnp.arange(N_TBL)[:, None] * SLOT_MAX + later).reshape(-1)
    padded = jnp.pad(place.reshape(N_TBL, PER_DEV), ((0, 0), (0, 8 - PER_DEV)), constant_values=-1).reshape(-1)
    wanted_second = (second[:, None] == padded[None, :]).astype(BF16)
    incident = lax.optimization_barrier(incidence.astype(BF16))
    gate_one = jnp.dot(low_one, lift_one, preferred_element_type=F32) + bias_one
    gate_zero = jnp.dot(low_zero, lift_zero, preferred_element_type=F32) + bias_zero
    gate_one, gate_zero, wanted, wanted_second = lax.optimization_barrier((gate_one, gate_zero, wanted, wanted_second))

    got = exchange(first_step(x_zero, grad_top, lift_one, squeeze_zero), TBL)
    rank_tile = jnp.sum(got[:, :16].astype(F32), axis=0).astype(BF16)
    part = jnp.dot(wanted_second, got[:, 16:].reshape(N_TBL * 8, 128), preferred_element_type=F32).astype(BF16)
    got = exchange(
        jnp.concatenate(
            [jnp.broadcast_to(rank_tile[None], (N_TBL, 16, 128)), part.reshape(N_TBL, SLOT_ROWS, 128)], axis=1
        ),
        TBL,
    )
    rank_one = from_tiles(got[:, :16])
    part = got[:, 16:]

    grad_mid = upstream + lax.dot_general(
        rank_one, squeeze_one, (((1,), (1,)), ((), ())), preferred_element_type=F32
    )
    part_zero = lax.dot_general(
        (grad_mid * embedded).astype(BF16), lift_zero, (((1,), (1,)), ((), ())), preferred_element_type=F32
    ).astype(BF16)
    pooled_local = (upstream * gate_one + grad_mid * gate_zero + grad_mid).astype(BF16)
    by_column = pooled_local.reshape(2, 128, PER_DEV, EMB).transpose(3, 0, 2, 1).reshape(N_TBL, 2 * PER_DEV, 128)
    send, part = lax.optimization_barrier((jnp.concatenate([to_tiles(part_zero), by_column], axis=1), part))
    got = exchange(send, TBL)
    part = part.reshape(32, 2, SLOT_ROWS, 128).transpose(2, 1, 0, 3).reshape(SLOT_MAX, 32, 128)
    other = lax.ppermute(part, "z", [(i, i ^ 2) for i in range(8)])
    got, part, other = lax.optimization_barrier((got, part, other))
    part = both(part, other, half, 1).reshape(SLOT_MAX * EMB, 128)
    rank_tile = jnp.sum(got[:, :16].astype(F32), axis=0).astype(BF16)

    placed = [
        jnp.dot(
            wanted,
            got[:, 16 + h * PER_DEV : 16 + (h + 1) * PER_DEV].reshape(FEATS, 128),
            preferred_element_type=F32,
        )
        .astype(BF16)
        .reshape(N_TBL, SLOT_MAX, 128)
        for h in range(2)
    ]
    send = jnp.concatenate([jnp.broadcast_to(rank_tile[None], (N_TBL, 16, 128))] + placed, axis=1)
    send, part = lax.optimization_barrier((send, part))
    got = exchange(send, TBL)
    parts = [part] + [lax.ppermute(part, REP, [(i, i ^ k) for i in range(N_REP)]) for k in (1, 2, 3)]
    for bit in (1, 2):
        parts = [jnp.where(quarter & bit == 0, parts[k], parts[k ^ bit]) for k in range(4)]
    squeeze_own = jnp.concatenate(parts, axis=1)
    rank_zero = from_tiles(got[:, :16])
    pooled_slots = (
        got[:, 16:].reshape(EMB, 2, SLOT_MAX, 128).transpose(2, 0, 1, 3).reshape(SLOT_MAX * EMB, ROWS)
    )
    pooled_slots = lax.optimization_barrier(pooled_slots)
    pooled = (
        pooled_slots.astype(F32)
        + lax.dot_general(
            squeeze_own,
            rank_zero,
            (((1,), (1,)), ((), ())),
            preferred_element_type=F32,
        )
    ).astype(BF16)
    partial = jnp.einsum(
        "sbu,seb->sue", incident, pooled.reshape(SLOT_MAX, EMB, ROWS), preferred_element_type=F32
    ).astype(BF16)

    share = TOUCH // N_REP
    got = exchange(partial.reshape(SLOT_MAX, N_REP, 4, 128).transpose(1, 0, 2, 3).reshape(N_REP, SLOT_MAX * 4, 128), REP)
    gradient = jnp.sum(got.astype(F32), axis=0).reshape(SLOT_MAX, 4, 2, EMB)
    history = lax.dynamic_slice(row_accum, (0, rep * share), (SLOT_MAX, share)).reshape(SLOT_MAX, 4, 2)
    history_new = history + jnp.mean(gradient * gradient, axis=3)
    update = LEARN_RATE * gradient / (jnp.sqrt(history_new)[:, :, :, None] + EPSILON)
    update = update.astype(BF16).reshape(SLOT_MAX * 4, 128)
    terms, rest = [], history_new.reshape(SLOT_MAX, share).T
    for _ in range(3):
        term = lax.reduce_precision(rest, 8, 7)
        terms.append(jnp.pad(term, ((0, 0), (0, 32 - SLOT_MAX))))
        rest = rest - term
    terms = jnp.pad(jnp.concatenate(terms, axis=1).astype(BF16), ((0, 0), (0, 32)))
    send = jnp.concatenate([update, terms], axis=0)
    return last_step(exchange(jnp.broadcast_to(send[None], (N_REP,) + send.shape), REP), table_rows)


def solution(mesh):
    grid = Mesh(mesh.devices.reshape(8, 8, 8, 2), TBL + REP)
    in_specs = (
        P(REP, TBL),
        P(REP, TBL),
        P(REP, None),
        P(REP, None),
        P(None, TBL),
        P(None, TBL),
        P(TBL, None),
        P(TBL, None),
        P(TBL),
        P(TBL),
        P(),
        P(),
        P(TBL, REP, None),
        P(TBL, None),
        P(TBL, None),
    )
    out_specs = (P(TBL, None), P(TBL, None))
    return jax.shard_map(shards, mesh=grid, in_specs=in_specs, out_specs=out_specs, check_vma=False)
```

time: 178 us -> 170 us (0.955)
  blocking collectives: 56.4 us -> 34.5 us
  starting transfers between devices: 61.4 us -> 80.6 us
  local copies, waits for them, and re-layouts: 10.4 us -> 5.33 us
  waiting for transfers between devices: 38.4 us -> 33.6 us
  Pallas kernels: 0 us -> 3.56 us
  other arithmetic: 4.21 us -> 7.31 us
  matrix products: 4.98 us -> 3.18 us
    all_to_all x3 -> x2, blocking collectives: 56.4 us -> 34.5 us  [exchange(): return lax.all_to_all(blocks, axis, split_axis=0, concat_axis=0, tiled=True)]
    all_to_all x3 -> x4, starting transfers between devices: 40.6 us -> 51.7 us  [exchange(): return lax.all_to_all(blocks, axis, split_axis=0, concat_axis=0, tiled=True)]
    ppermute x2 -> x4, starting transfers between devices: 20.8 us -> 28.9 us  [the longest x1 14.8 us: shards(): other = lax.ppermute(part, 'z', [(i, i ^ 2) for i in range(8)])]
    pallas_call x0 -> x2, Pallas kernels: none -> 3.56 us  [the longest x1 2.55 us: first_step(): pl.pallas_call(first_kernel, out_shape=jax.ShapeDtypeStruct((N_TBL, 24, 1...]
    ppermute x2 -> x4, waiting for transfers between devices: 12.8 us -> 9.46 us  [the longest x3 6.68 us: shards(): lax.ppermute(part, REP, [(i, i ^ k) for i in range(N_REP)])]
    unnamed x33 -> x36, local copies, waits for them, and re-layouts: 3.47 us -> 0.77 us
    convert_element_type x2 -> x3, other arithmetic: 0.16 us -> 2.41 us  [the longest x1 1.92 us: shards(): incident = lax.optimization_barrier(incidence.astype(BF16))]
    all_to_all x3 -> x4, waiting for transfers between devices: 25.7 us -> 24.1 us  [exchange(): return lax.all_to_all(blocks, axis, split_axis=0, concat_axis=0, tiled=True)]
  transfers between devices with their start and end apart: 5 -> 8, of which waited for: 4 -> 4; matrix products, arithmetic and copies ran while one was open for 1% -> 3% of each run, Pallas kernels for 0% -> 0%
where the time goes in v3:
time: 170 us; the launch traced here: 169 us
  starting transfers between devices  80.6 us (47%)
  blocking collectives  34.5 us (20%)
  waiting for transfers between devices  33.6 us (20%)
  other arithmetic  7.31 us (4%)
  local copies, waits for them, and re-layouts  5.33 us (3%)
  Pallas kernels  3.56 us (2%)
  matrix products  3.18 us (2%)
    all_to_all x4, starting transfers between devices, exchange(): return lax.all_to_all(blocks, axis, split_axis=0, concat_axis=0, tiled=True)  51.7 us
    all_to_all x2, blocking collectives, exchange(): return lax.all_to_all(blocks, axis, split_axis=0, concat_axis=0, tiled=True)  34.5 us
    all_to_all x4, waiting for transfers between devices, exchange(): return lax.all_to_all(blocks, axis, split_axis=0, concat_axis=0, tiled=True)  24.1 us
    ppermute x1, starting transfers between devices, shards(): other = lax.ppermute(part, 'z', [(i, i ^ 2) for i in range(8)])  14.8 us
    ppermute x3, starting transfers between devices, shards(): lax.ppermute(part, REP, [(i, i ^ k) for i in range(N_REP)])  14.1 us
    ppermute x3, waiting for transfers between devices, shards(): lax.ppermute(part, REP, [(i, i ^ k) for i in range(N_REP)])  6.68 us
  transfers between devices with their start and end apart: 8, of which 4 were waited for; matrix products, arithmetic and copies ran while one was open for 3% of the time, Pallas kernels for 0%

profile of v3, /device:TPU:1, one launch (start us, length us, event | category | flops | bytes accessed | tf_op | source)
XLA Modules:
  0.0 169.5 jit_solution(17508994097585967481)
XLA Ops:
  0.7 2.5 %first_step.1 = bf16[64,24,128]{2,1,0:T(8,128)(2,1)} custom-call(bf16[256,384]{1,0:T(8,128)(2,1)} %x_hbm.1, bf16[256,384]{1,0:T(8,128)(2,1)} %top_hbm.1, bf16[512,384]{1,0:T(8,128)(2,1)} %lift_hbm.1, bf16[384,512]{1,0:T(8,128)(2,1)} %squeeze_hbm.1), custom_call_target="tpu_custom_call" | custom-call | tf_op jit(solution)/shard_map/first_step/pallas_call | solution.py:74
  3.3 14.0 %all-to-all-start = ((bf16[64,24,128]{2,1,0:T(8,128)(2,1)}), bf16[64,24,128]{2,1,0:T(8,128)(2,1)S(1)}, u32[]{:S(2)}, u32[]{:S(2)}) async-start(bf16[64,24,128]{2,1,0:T(8,128)(2,1)} %first_step.1), calls=%async_computation | async-start | bytes 786432 | tf_op jit(solution)/shard_map/all_to_all | solution.py:31
  17.4 0.1 add.124
  17.6 0.1 reshape.128
  17.9 0.3 convolution_add_fusion.3
  18.2 0.2 compare_convert_fusion
  18.4 0.3 convolution_add_fusion.2
  18.7 0.3 fusion.1
  19.0 11.9 %all-to-all-done = bf16[64,24,128]{2,1,0:T(8,128)(2,1)S(1)} async-done(((bf16[64,24,128]{2,1,0:T(8,128)(2,1)}), bf16[64,24,128]{2,1,0:T(8,128)(2,1)S(1)}, u32[]{:S(2)}, u32[]{:S(2)}) %all-to-all-start) | async-done | bytes 393248 | tf_op jit(solution)/shard_map/all_to_all | solution.py:31
  30.9 0.3 convolution_convert_fusion.4
  31.5 18.7 %all_to_all.30 = bf16[64,25,128]{2,1,0:T(8,128)(2,1)S(1)} all-to-all(bf16[64,25,128]{2,1,0:T(8,128)(2,1)S(1)} %pad_maximum_fusion.1), channel_id=1, replica_groups=mesh['y'=8,'x'=8,'z'=8,'core'=2] {'y','x'}, dimensions={0} | all-to-all | bytes 819200 | tf_op jit(solution)/shard_map/all_to_all | solution.py:31
  50.3 0.1 copy.60
  50.4 0.3 fusion.12
  50.8 0.1 copy.62
  51.0 0.1 copy.64
  51.2 0.2 copy-done.4
  51.3 0.3 convolution_convert_fusion.3
  51.8 0.9 pad_maximum_fusion.2
  52.7 4.9 %all-to-all-start.2 = ((bf16[64,28,128]{2,1,0:T(8,128)(2,1)}), bf16[64,28,128]{2,1,0:T(8,128)(2,1)S(1)}, u32[]{:S(2)}, u32[]{:S(2)}) async-start(bf16[64,28,128]{2,1,0:T(8,128)(2,1)} %pad_maximum_fusion.2), calls=%async_computation.2 | async-start | bytes 1048576 | tf_op jit(solution)/shard_map/all_to_all | solution.py:31
  57.7 14.8 %collective-permute-start = (bf16[18,32,128]{2,1,0:T(8,128)(2,1)S(1)}, bf16[18,32,128]{2,1,0:T(8,128)(2,1)S(1)}, u32[]{:S(2)}, u32[]{:S(2)}) collective-permute-start(bf16[18,32,128]{2,1,0:T(8,128)(2,1)S(1)} %bitcast.83), channel_id=1, source_target_pairs={{0,4},{2,6},{4,0},{6,2},{8,12},{10,14},{12,8},{14,10},{1,5},{3,7},... | collective-permute-start | bytes 442376 | tf_op jit(solution)/shard_map/ppermute | solution.py:181
  72.5 2.8 %collective-permute-done = bf16[18,32,128]{2,1,0:T(8,128)(2,1)S(1)} collective-permute-done((bf16[18,32,128]{2,1,0:T(8,128)(2,1)S(1)}, bf16[18,32,128]{2,1,0:T(8,128)(2,1)S(1)}, u32[]{:S(2)}, u32[]{:S(2)}) %collective-permute-start) | collective-permute-done | bytes 147488 | tf_op jit(solution)/shard_map/ppermute | solution.py:181
  75.6 0.4 convolution_convert_fusion
  75.9 0.4 convolution_convert_fusion.1
  76.5 0.1 maximum_select_fusion
  76.7 1.1 pad_maximum_fusion
  77.8 11.8 %all-to-all-start.3 = ((bf16[64,52,128]{2,1,0:T(8,128)(2,1)}), bf16[64,52,128]{2,1,0:T(8,128)(2,1)S(1)}, u32[]{:S(2)}, u32[]{:S(2)}) async-start(bf16[64,52,128]{2,1,0:T(8,128)(2,1)} %pad_maximum_fusion), calls=%async_computation.3 | async-start | bytes 1835008 | tf_op jit(solution)/shard_map/all_to_all | solution.py:31
  89.7 8.6 %collective-permute-start.3 = (bf16[1152,128]{1,0:T(8,128)(2,1)S(1)}, bf16[1152,128]{1,0:T(8,128)(2,1)S(1)}, u32[]{:S(2)}, u32[]{:S(2)}) collective-permute-start(bf16[1152,128]{1,0:T(8,128)(2,1)S(1)} %bitcast.71), channel_id=1, source_target_pairs={{0,3},{1,2},{2,1},{3,0},{4,7},{5,6},{6,5},{7,4},{8,11},{9,10},{10,... | collective-permute-start | bytes 884744 | tf_op jit(solution)/shard_map/ppermute | solution.py:199
  98.3 3.4 %collective-permute-start.2 = (bf16[1152,128]{1,0:T(8,128)(2,1)S(1)}, bf16[1152,128]{1,0:T(8,128)(2,1)S(1)}, u32[]{:S(2)}, u32[]{:S(2)}) collective-permute-start(bf16[1152,128]{1,0:T(8,128)(2,1)S(1)} %bitcast.72), channel_id=1, source_target_pairs={{0,2},{1,3},{2,0},{3,1},{4,6},{5,7},{6,4},{7,5},{8,10},{9,11},{10,... | collective-permute-start | bytes 884744 | tf_op jit(solution)/shard_map/ppermute | solution.py:199
  101.7 2.1 %collective-permute-start.1 = (bf16[1152,128]{1,0:T(8,128)(2,1)S(1)}, bf16[1152,128]{1,0:T(8,128)(2,1)}, u32[]{:S(2)}, u32[]{:S(2)}) collective-permute-start(bf16[1152,128]{1,0:T(8,128)(2,1)S(1)} %bitcast.73), channel_id=1, source_target_pairs={{0,1},{1,0},{2,3},{3,2},{4,5},{5,4},{6,7},{7,6},{8,9},{9,8},{10,11... | collective-permute-start | bytes 884744 | tf_op jit(solution)/shard_map/ppermute | solution.py:199
  103.9 1.9 %convert_element_type.75 = bf16[18,256,128]{2,1,0:T(8,128)(2,1)S(1)} convert(s32[18,256,128]{2,1,0:T(8,128)} %param.27) | non-fusion elementwise | flops 589824 | bytes 3538944 | tf_op jit(solution)/shard_map/convert_element_type | solution.py:153
  105.8 6.7 %collective-permute-done.2 = bf16[1152,128]{1,0:T(8,128)(2,1)S(1)} collective-permute-done((bf16[1152,128]{1,0:T(8,128)(2,1)S(1)}, bf16[1152,128]{1,0:T(8,128)(2,1)S(1)}, u32[]{:S(2)}, u32[]{:S(2)}) %collective-permute-start.2) | collective-permute-done | bytes 294944 | tf_op jit(solution)/shard_map/ppermute | solution.py:199
  112.5 2.1 %broadcast_select_fusion.7 = (bf16[1152,128]{1,0:T(8,128)(2,1)}, bf16[1152,128]{1,0:T(8,128)(2,1)}, bf16[1152,128]{1,0:T(8,128)(2,1)}, bf16[1152,128]{1,0:T(8,128)(2,1)}) fusion(pred[]{:T(512)S(6)} %eq.55, bf16[1152,128]{1,0:T(8,128)(2,1)S(1)} %bitcast.74, bf16[1152,128]{1,0:T(8,128)(2,1)} %collective-permute-done.1, pred[]{:T(512)S(6)} %eq.56, ...), kind=kLoop, calls=%fused_computation.39 | loop fusion | flops 1179648 | bytes 2359298 | tf_op jit(solution)/shard_map/jit(_where)/select_n | solution.py:201
  114.7 0.1 copy.67
  114.8 0.6 copy.68
  115.6 0.1 copy.69
  116.0 0.5 fusion
  116.5 0.3 fusion.9
  116.9 0.3 copy.70
  117.2 0.3 reshape.148
  117.6 0.8 copy.72
  118.4 20.9 %all-to-all-start.4 = ((bf16[16,72,128]{2,1,0:T(8,128)(2,1)}), bf16[16,72,128]{2,1,0:T(8,128)(2,1)S(1)}, u32[]{:S(2)}, u32[]{:S(2)}) async-start(bf16[16,72,128]{2,1,0:T(8,128)(2,1)} %copy.72), calls=%async_computation.4 | async-start | bytes 589824 | tf_op jit(solution)/shard_map/all_to_all | solution.py:31
  139.4 12.2 %all-to-all-done.4 = bf16[16,72,128]{2,1,0:T(8,128)(2,1)S(1)} async-done(((bf16[16,72,128]{2,1,0:T(8,128)(2,1)}), bf16[16,72,128]{2,1,0:T(8,128)(2,1)S(1)}, u32[]{:S(2)}, u32[]{:S(2)}) %all-to-all-start.4) | async-done | bytes 294944 | tf_op jit(solution)/shard_map/all_to_all | solution.py:31
  151.8 0.2 reduce_sum.45
  152.0 0.1 copy.74
  152.1 0.1 copy.76
  152.2 0.1 div.32
  152.6 15.8 %all_to_all.31.got_ref = bf16[16,80,128]{2,1,0:T(8,128)(2,1)S(1)} all-to-all(bf16[16,80,128]{2,1,0:T(8,128)(2,1)S(1)} %broadcast_in_dim.8), channel_id=1, replica_groups=mesh['y'=8,'x'=8,'z'=8,'core'=2] {'z','core'}, dimensions={0} | all-to-all | bytes 655360 | tf_op jit(solution)/shard_map/all_to_all | solution.py:31
  168.4 1.0 last_step.1
  (79 shorter events, 2.4 us)
Async XLA Ops:
  0.6 17.7 %copy-start = (bf16[512,384]{1,0:T(8,128)(2,1)S(1)}, bf16[512,384]{1,0:T(8,128)(2,1)}, u32[]{:S(2)}) copy-start(bf16[512,384]{1,0:T(8,128)(2,1)} %param.19) | copy-start | bytes 1179652
  0.6 17.2 %copy-start.2 = (bf16[512,384]{1,0:T(8,128)(2,1)S(1)}, bf16[512,384]{1,0:T(8,128)(2,1)}, u32[]{:S(2)}) copy-start(bf16[512,384]{1,0:T(8,128)(2,1)} %lift_hbm.1) | copy-start | bytes 1179652
  0.7 16.9 %copy-start.15 = (s32[384]{0:T(512)S(1)}, s32[384]{0:T(512)}, u32[]{:S(2)}) copy-start(s32[384]{0:T(512)} %param.26) | copy-start | bytes 4612
  0.7 16.9 %copy-start.16 = (s32[384]{0:T(512)S(1)}, s32[384]{0:T(512)}, u32[]{:S(2)}) copy-start(s32[384]{0:T(512)} %param.25) | copy-start | bytes 4612
  0.7 17.2 %copy-start.13 = (f32[384]{0:T(512)S(1)}, f32[384]{0:T(512)}, u32[]{:S(2)}) copy-start(f32[384]{0:T(512)} %param.24) | copy-start | bytes 4612
  0.7 17.2 %copy-start.10 = (bf16[256,512]{1,0:T(8,128)(2,1)S(1)}, bf16[256,512]{1,0:T(8,128)(2,1)}, u32[]{:S(2)}) copy-start(bf16[256,512]{1,0:T(8,128)(2,1)} %param.18) | copy-start | bytes 786436
  0.7 17.7 %copy-start.14 = (f32[384]{0:T(512)S(1)}, f32[384]{0:T(512)}, u32[]{:S(2)}) copy-start(f32[384]{0:T(512)} %param.23) | copy-start | bytes 4612
  0.7 17.7 %copy-start.11 = (bf16[256,512]{1,0:T(8,128)(2,1)S(1)}, bf16[256,512]{1,0:T(8,128)(2,1)}, u32[]{:S(2)}) copy-start(bf16[256,512]{1,0:T(8,128)(2,1)} %param.17) | copy-start | bytes 786436
  3.3 27.6 %all-to-all-start = ((bf16[64,24,128]{2,1,0:T(8,128)(2,1)}), bf16[64,24,128]{2,1,0:T(8,128)(2,1)S(1)}, u32[]{:S(2)}, u32[]{:S(2)}) async-start(bf16[64,24,128]{2,1,0:T(8,128)(2,1)} %first_step.1), calls=%async_computation | async-start | bytes 786432 | tf_op jit(solution)/shard_map/all_to_all | solution.py:31
  31.4 19.0 %copy-start.3 = (bf16[256,384]{1,0:T(8,128)(2,1)S(1)}, bf16[256,384]{1,0:T(8,128)(2,1)}, u32[]{:S(2)}) copy-start(bf16[256,384]{1,0:T(8,128)(2,1)} %top_hbm.1) | copy-start | bytes 589828
  31.4 19.0 %copy-start.5 = (bf16[384,512]{1,0:T(8,128)(2,1)S(1)}, bf16[384,512]{1,0:T(8,128)(2,1)}, u32[]{:S(2)}) copy-start(bf16[384,512]{1,0:T(8,128)(2,1)} %param.22) | copy-start | bytes 1179652
  50.4 0.9 copy-start.4
  52.7 22.6 %all-to-all-start.2 = ((bf16[64,28,128]{2,1,0:T(8,128)(2,1)}), bf16[64,28,128]{2,1,0:T(8,128)(2,1)S(1)}, u32[]{:S(2)}, u32[]{:S(2)}) async-start(bf16[64,28,128]{2,1,0:T(8,128)(2,1)} %pad_maximum_fusion.2), calls=%async_computation.2 | async-start | bytes 1048576 | tf_op jit(solution)/shard_map/all_to_all | solution.py:31
  57.7 17.6 %collective-permute-start = (bf16[18,32,128]{2,1,0:T(8,128)(2,1)S(1)}, bf16[18,32,128]{2,1,0:T(8,128)(2,1)S(1)}, u32[]{:S(2)}, u32[]{:S(2)}) collective-permute-start(bf16[18,32,128]{2,1,0:T(8,128)(2,1)S(1)} %bitcast.83), channel_id=1, source_target_pairs={{0,4},{2,6},{4,0},{6,2},{8,12},{10,14},{12,8},{14,10},{1,5},{3,7},... | collective-permute-start | bytes 442376 | tf_op jit(solution)/shard_map/ppermute | solution.py:181
  77.8 36.7 %all-to-all-start.3 = ((bf16[64,52,128]{2,1,0:T(8,128)(2,1)}), bf16[64,52,128]{2,1,0:T(8,128)(2,1)S(1)}, u32[]{:S(2)}, u32[]{:S(2)}) async-start(bf16[64,52,128]{2,1,0:T(8,128)(2,1)} %pad_maximum_fusion), calls=%async_computation.3 | async-start | bytes 1835008 | tf_op jit(solution)/shard_map/all_to_all | solution.py:31
  89.7 16.1 %collective-permute-start.3 = (bf16[1152,128]{1,0:T(8,128)(2,1)S(1)}, bf16[1152,128]{1,0:T(8,128)(2,1)S(1)}, u32[]{:S(2)}, u32[]{:S(2)}) collective-permute-start(bf16[1152,128]{1,0:T(8,128)(2,1)S(1)} %bitcast.71), channel_id=1, source_target_pairs={{0,3},{1,2},{2,1},{3,0},{4,7},{5,6},{6,5},{7,4},{8,11},{9,10},{10,... | collective-permute-start | bytes 884744 | tf_op jit(solution)/shard_map/ppermute | solution.py:199
  98.3 14.2 %collective-permute-start.2 = (bf16[1152,128]{1,0:T(8,128)(2,1)S(1)}, bf16[1152,128]{1,0:T(8,128)(2,1)S(1)}, u32[]{:S(2)}, u32[]{:S(2)}) collective-permute-start(bf16[1152,128]{1,0:T(8,128)(2,1)S(1)} %bitcast.72), channel_id=1, source_target_pairs={{0,2},{1,3},{2,0},{3,1},{4,6},{5,7},{6,4},{7,5},{8,10},{9,11},{10,... | collective-permute-start | bytes 884744 | tf_op jit(solution)/shard_map/ppermute | solution.py:199
  101.7 10.7 %collective-permute-start.1 = (bf16[1152,128]{1,0:T(8,128)(2,1)S(1)}, bf16[1152,128]{1,0:T(8,128)(2,1)}, u32[]{:S(2)}, u32[]{:S(2)}) collective-permute-start(bf16[1152,128]{1,0:T(8,128)(2,1)S(1)} %bitcast.73), channel_id=1, source_target_pairs={{0,1},{1,0},{2,3},{3,2},{4,5},{5,4},{6,7},{7,6},{8,9},{9,8},{10,11... | collective-permute-start | bytes 884744 | tf_op jit(solution)/shard_map/ppermute | solution.py:199
  114.8 1.0 copy-start.6
  114.8 1.0 copy-start.7
  114.8 1.1 copy-start.8
  114.8 1.2 copy-start.9
  116.9 22.3 %copy-start.12 = (f32[18,128]{1,0:T(8,128)S(1)}, f32[18,128]{1,0:T(8,128)}, u32[]{:S(2)}) copy-start(f32[18,128]{1,0:T(8,128)} %param.29) | copy-start | bytes 27652
  117.6 50.9 %copy-start.1 = (f32[18,8192]{1,0:T(8,128)S(1)}, f32[18,8192]{1,0:T(8,128)}, u32[]{:S(2)}) copy-start(f32[18,8192]{1,0:T(8,128)} %rows_ref.1) | copy-start | bytes 1769476
  118.4 33.2 %all-to-all-start.4 = ((bf16[16,72,128]{2,1,0:T(8,128)(2,1)}), bf16[16,72,128]{2,1,0:T(8,128)(2,1)S(1)}, u32[]{:S(2)}, u32[]{:S(2)}) async-start(bf16[16,72,128]{2,1,0:T(8,128)(2,1)} %copy.72), calls=%async_computation.4 | async-start | bytes 589824 | tf_op jit(solution)/shard_map/all_to_all | solution.py:31

commit v4 on v3

--- a/solution.py
+++ b/solution.py
@@ -29,6 +29,15 @@
 
 def exchange(blocks, axis):
     return lax.all_to_all(blocks, axis, split_axis=0, concat_axis=0, tiled=True)
+
+
+def exchange_rows(parts, axis):
+    blocks, rows = parts[0].shape[0], sum(part.shape[1] for part in parts)
+    spare = -rows % 4
+    if spare:
+        parts = parts + [jnp.zeros((blocks, spare, 128), BF16)]
+    sent = jnp.concatenate(parts, axis=1).reshape(blocks, (rows + spare) // 4, 4, 128)
+    return sent, lambda sent: exchange(sent, axis).reshape(blocks, rows + spare, 128)[:, :rows]
 
 
 def to_tiles(matrix):
@@ -158,12 +167,10 @@
     got = exchange(first_step(x_zero, grad_top, lift_one, squeeze_zero), TBL)
     rank_tile = jnp.sum(got[:, :16].astype(F32), axis=0).astype(BF16)
     part = jnp.dot(wanted_second, got[:, 16:].reshape(N_TBL * 8, 128), preferred_element_type=F32).astype(BF16)
-    got = exchange(
-        jnp.concatenate(
-            [jnp.broadcast_to(rank_tile[None], (N_TBL, 16, 128)), part.reshape(N_TBL, SLOT_ROWS, 128)], axis=1
-        ),
-        TBL,
-    )
+    send, move = exchange_rows(
+        [jnp.broadcast_to(rank_tile[None], (N_TBL, 16, 128)), part.reshape(N_TBL, SLOT_ROWS, 128)], TBL
+    )
+    got = move(send)
     rank_one = from_tiles(got[:, :16])
     part = got[:, 16:]
 
@@ -175,8 +182,9 @@
     ).astype(BF16)
     pooled_local = (upstream * gate_one + grad_mid * gate_zero + grad_mid).astype(BF16)
     by_column = pooled_local.reshape(2, 128, PER_DEV, EMB).transpose(3, 0, 2, 1).reshape(N_TBL, 2 * PER_DEV, 128)
-    send, part = lax.optimization_barrier((jnp.concatenate([to_tiles(part_zero), by_column], axis=1), part))
-    got = exchange(send, TBL)
+    send, move = exchange_rows([to_tiles(part_zero), by_column], TBL)
+    send, part = lax.optimization_barrier((send, part))
+    got = move(send)
     part = part.reshape(32, 2, SLOT_ROWS, 128).transpose(2, 1, 0, 3).reshape(SLOT_MAX, 32, 128)
     other = lax.ppermute(part, "z", [(i, i ^ 2) for i in range(8)])
     got, part, other = lax.optimization_barrier((got, part, other))
@@ -193,14 +201,16 @@
         .reshape(N_TBL, SLOT_MAX, 128)
         for h in range(2)
     ]
-    send = jnp.concatenate([jnp.broadcast_to(rank_tile[None], (N_TBL, 16, 128))] + placed, axis=1)
+    send, move = exchange_rows([jnp.broadcast_to(rank_tile[None], (N_TBL, 16, 128))] + placed, TBL)
     send, part = lax.optimization_barrier((send, part))
-    got = exchange(send, TBL)
+    got = move(send)
     parts = [part] + [lax.ppermute(part, REP, [(i, i ^ k) for i in range(N_REP)]) for k in (1, 2, 3)]
+    squeeze_own = jnp.concatenate(parts, axis=1)
+    tiles = got[:, :16].reshape(16, 4, 16, 128)
+    blocks = [tiles[:, k] for k in range(4)]
     for bit in (1, 2):
-        parts = [jnp.where(quarter & bit == 0, parts[k], parts[k ^ bit]) for k in range(4)]
-    squeeze_own = jnp.concatenate(parts, axis=1)
-    rank_zero = from_tiles(got[:, :16])
+        blocks = [jnp.where(quarter & bit == 0, blocks[k], blocks[k ^ bit]) for k in range(4)]
+    rank_zero = jnp.concatenate([block.reshape(ROWS, 128) for block in blocks], axis=1)
     pooled_slots = (
         got[:, 16:].reshape(EMB, 2, SLOT_MAX, 128).transpose(2, 0, 1, 3).reshape(SLOT_MAX * EMB, ROWS)
     )

time: 170 us -> 170 us (level)
  starting transfers between devices: 80.6 us -> 76.6 us
  local copies, waits for them, and re-layouts: 5.33 us -> 9.11 us
  other arithmetic: 7.31 us -> 3.66 us
  waiting for transfers between devices: 33.6 us -> 36.5 us
    all_to_all x4, starting transfers between devices: 51.7 us -> 48.1 us  [exchange(): return lax.all_to_all(blocks, axis, split_axis=0, concat_axis=0, tiled=True)]
    optimization_barrier x1 -> x2, local copies, waits for them, and re-layouts: 0.04 us -> 2.68 us  [shards(): send, part = lax.optimization_barrier((send, part))]
    select_n x1 -> x2, other arithmetic: 2.12 us -> 0.18 us  [shards(): jnp.where(quarter & bit == 0, blocks[k], blocks[k ^ bit])]
    concatenate x3, other arithmetic: 2.07 us -> 0.37 us  [exchange_rows(): jnp.concatenate(parts, axis=1).reshape(blocks, (rows + spare) // 4, 4, 128)]
  transfers between devices with their start and end apart: 8 -> 8, of which waited for: 4 -> 6; matrix products, arithmetic and copies ran while one was open for 3% -> 3% of each run, Pallas kernels for 0% -> 0%
where the time goes in v4:
time: 170 us; the launch traced here: 169 us
  starting transfers between devices  76.6 us (45%)
  waiting for transfers between devices  36.5 us (21%)
  blocking collectives  34.1 us (20%)
  local copies, waits for them, and re-layouts  9.11 us (5%)
  matrix products  4.14 us (2%)
  other arithmetic  3.66 us (2%)
  Pallas kernels  3.56 us (2%)
    all_to_all x4, starting transfers between devices, exchange(): return lax.all_to_all(blocks, axis, split_axis=0, concat_axis=0, tiled=True)  48.1 us
    all_to_all x2, blocking collectives, exchange(): return lax.all_to_all(blocks, axis, split_axis=0, concat_axis=0, tiled=True)  34.1 us
    all_to_all x4, waiting for transfers between devices, exchange(): return lax.all_to_all(blocks, axis, split_axis=0, concat_axis=0, tiled=True)  25.8 us
    ppermute x3, starting transfers between devices, shards(): lax.ppermute(part, REP, [(i, i ^ k) for i in range(N_REP)])  14.3 us
    ppermute x1, starting transfers between devices, shards(): other = lax.ppermute(part, 'z', [(i, i ^ 2) for i in range(8)])  14.2 us
    ppermute x3, waiting for transfers between devices, shards(): lax.ppermute(part, REP, [(i, i ^ k) for i in range(N_REP)])  8.03 us
  transfers between devices with their start and end apart: 8, of which 6 were waited for; matrix products, arithmetic and copies ran while one was open for 3% of the time, Pallas kernels for 0%

profile of v4, /device:TPU:1, one launch (start us, length us, event | category | flops | bytes accessed | tf_op | source)
XLA Modules:
  0.0 169.1 jit_solution(2414179917778065966)
XLA Ops:
  0.7 2.5 %first_step.1 = bf16[64,24,128]{2,1,0:T(8,128)(2,1)} custom-call(bf16[256,384]{1,0:T(8,128)(2,1)} %x_hbm.1, bf16[256,384]{1,0:T(8,128)(2,1)} %top_hbm.1, bf16[512,384]{1,0:T(8,128)(2,1)} %lift_hbm.1, bf16[384,512]{1,0:T(8,128)(2,1)} %squeeze_hbm.1), custom_call_target="tpu_custom_call" | custom-call | tf_op jit(solution)/shard_map/first_step/pallas_call | solution.py:83
  3.3 14.0 %all-to-all-start = ((bf16[64,24,128]{2,1,0:T(8,128)(2,1)}), bf16[64,24,128]{2,1,0:T(8,128)(2,1)S(1)}, u32[]{:S(2)}, u32[]{:S(2)}) async-start(bf16[64,24,128]{2,1,0:T(8,128)(2,1)} %first_step.1), calls=%async_computation | async-start | bytes 786432 | tf_op jit(solution)/shard_map/all_to_all | solution.py:31
  17.9 0.3 convolution_add_fusion.3
  18.2 0.2 compare_convert_fusion
  18.4 0.3 convolution_add_fusion.2
  18.7 0.3 fusion.1
  19.1 11.8 %all-to-all-done = bf16[64,24,128]{2,1,0:T(8,128)(2,1)S(1)} async-done(((bf16[64,24,128]{2,1,0:T(8,128)(2,1)}), bf16[64,24,128]{2,1,0:T(8,128)(2,1)S(1)}, u32[]{:S(2)}, u32[]{:S(2)}) %all-to-all-start) | async-done | bytes 393248 | tf_op jit(solution)/shard_map/all_to_all | solution.py:31
  30.9 0.3 convolution_convert_fusion.4
  31.6 0.4 copy.83
  32.0 18.3 %all_to_all.30 = bf16[64,7,4,128]{3,2,1,0:T(4,128)(2,1)S(1)} all-to-all(bf16[64,7,4,128]{3,2,1,0:T(4,128)(2,1)S(1)} %copy.83), channel_id=1, replica_groups=mesh['y'=8,'x'=8,'z'=8,'core'=2] {'y','x'}, dimensions={0} | all-to-all | bytes 917504 | tf_op jit(solution)/shard_map/all_to_all | solution.py:31
  50.6 0.3 fusion.12
  50.9 0.1 copy.87
  51.1 0.1 copy.89
  51.3 0.2 copy-done.4
  51.5 0.3 convolution_convert_fusion.3
  52.0 0.2 copy.90
  52.2 1.1 copy.91
  53.3 4.6 %all-to-all-start.2 = ((bf16[64,7,4,128]{3,2,1,0:T(4,128)(2,1)}), bf16[64,7,4,128]{3,2,1,0:T(4,128)(2,1)S(1)}, u32[]{:S(2)}, u32[]{:S(2)}) async-start(bf16[64,7,4,128]{3,2,1,0:T(4,128)(2,1)} %copy.91), calls=%async_computation.2 | async-start | bytes 917504 | tf_op jit(solution)/shard_map/all_to_all | solution.py:31
  58.0 14.2 %collective-permute-start = (bf16[18,32,128]{2,1,0:T(8,128)(2,1)S(1)}, bf16[18,32,128]{2,1,0:T(8,128)(2,1)S(1)}, u32[]{:S(2)}, u32[]{:S(2)}) collective-permute-start(bf16[18,32,128]{2,1,0:T(8,128)(2,1)S(1)} %bitcast.91), channel_id=1, source_target_pairs={{0,4},{2,6},{4,0},{6,2},{8,12},{10,14},{12,8},{14,10},{1,5},{3,7},... | collective-permute-start | bytes 442376 | tf_op jit(solution)/shard_map/ppermute | solution.py:189
  72.3 2.7 %collective-permute-done = bf16[18,32,128]{2,1,0:T(8,128)(2,1)S(1)} collective-permute-done((bf16[18,32,128]{2,1,0:T(8,128)(2,1)S(1)}, bf16[18,32,128]{2,1,0:T(8,128)(2,1)S(1)}, u32[]{:S(2)}, u32[]{:S(2)}) %collective-permute-start) | collective-permute-done | bytes 147488 | tf_op jit(solution)/shard_map/ppermute | solution.py:189
  75.2 0.4 convolution_convert_fusion.1
  75.8 0.4 convolution_convert_fusion
  76.4 0.2 pad_maximum_fusion
  76.6 0.2 copy.96
  76.9 1.6 copy.97
  78.5 11.8 %all-to-all-start.3 = ((bf16[64,13,4,128]{3,2,1,0:T(4,128)(2,1)}), bf16[64,13,4,128]{3,2,1,0:T(4,128)(2,1)S(1)}, u32[]{:S(2)}, u32[]{:S(2)}) async-start(bf16[64,13,4,128]{3,2,1,0:T(4,128)(2,1)} %copy.97), calls=%async_computation.3 | async-start | bytes 1703936 | tf_op jit(solution)/shard_map/all_to_all | solution.py:31
  90.3 1.9 %convert_element_type.75 = bf16[18,256,128]{2,1,0:T(8,128)(2,1)S(1)} convert(s32[18,256,128]{2,1,0:T(8,128)} %param.27) | non-fusion elementwise | flops 589824 | bytes 3538944 | tf_op jit(solution)/shard_map/convert_element_type | solution.py:162
  92.3 8.7 %collective-permute-start.1 = (bf16[1152,128]{1,0:T(8,128)(2,1)S(1)}, bf16[1152,128]{1,0:T(8,128)(2,1)S(1)}, u32[]{:S(2)}, u32[]{:S(2)}) collective-permute-start(bf16[1152,128]{1,0:T(8,128)(2,1)S(1)} %bitcast.94), channel_id=1, source_target_pairs={{0,1},{1,0},{2,3},{3,2},{4,5},{5,4},{6,7},{7,6},{8,9},{9,8},{10,11... | collective-permute-start | bytes 884744 | tf_op jit(solution)/shard_map/ppermute | solution.py:207
  101.0 1.9 %collective-permute-start.2 = (bf16[1152,128]{1,0:T(8,128)(2,1)S(1)}, bf16[1152,128]{1,0:T(8,128)(2,1)S(1)}, u32[]{:S(2)}, u32[]{:S(2)}) collective-permute-start(bf16[1152,128]{1,0:T(8,128)(2,1)S(1)} %bitcast.95), channel_id=1, source_target_pairs={{0,2},{1,3},{2,0},{3,1},{4,6},{5,7},{6,4},{7,5},{8,10},{9,11},{10,... | collective-permute-start | bytes 884744 | tf_op jit(solution)/shard_map/ppermute | solution.py:207
  102.9 3.7 %collective-permute-start.3 = (bf16[1152,128]{1,0:T(8,128)(2,1)S(1)}, bf16[1152,128]{1,0:T(8,128)(2,1)}, u32[]{:S(2)}, u32[]{:S(2)}) collective-permute-start(bf16[1152,128]{1,0:T(8,128)(2,1)S(1)} %bitcast.96), channel_id=1, source_target_pairs={{0,3},{1,2},{2,1},{3,0},{4,7},{5,6},{6,5},{7,4},{8,11},{9,10},{10,... | collective-permute-start | bytes 884744 | tf_op jit(solution)/shard_map/ppermute | solution.py:207
  106.6 1.8 %all-to-all-done.3 = bf16[64,13,4,128]{3,2,1,0:T(4,128)(2,1)S(1)} async-done(((bf16[64,13,4,128]{3,2,1,0:T(4,128)(2,1)}), bf16[64,13,4,128]{3,2,1,0:T(4,128)(2,1)S(1)}, u32[]{:S(2)}, u32[]{:S(2)}) %all-to-all-start.3) | async-done | bytes 852000 | tf_op jit(solution)/shard_map/all_to_all | solution.py:31
  108.4 0.2 copy.98
  108.6 0.4 fusion.36
  109.0 0.2 broadcast_select_fusion.7
  109.2 0.6 copy.99
  110.0 1.5 collective-permute-done.2
  111.5 6.5 %collective-permute-done.3 = bf16[1152,128]{1,0:T(8,128)(2,1)} collective-permute-done((bf16[1152,128]{1,0:T(8,128)(2,1)S(1)}, bf16[1152,128]{1,0:T(8,128)(2,1)}, u32[]{:S(2)}, u32[]{:S(2)}) %collective-permute-start.3) | collective-permute-done | bytes 294944 | tf_op jit(solution)/shard_map/ppermute | solution.py:207
  118.0 1.5 fusion
  119.5 0.3 fusion.9
  119.8 0.3 copy.104
  120.2 0.3 reshape.204
  120.5 0.8 copy.106
  121.3 17.6 %all-to-all-start.4 = ((bf16[16,72,128]{2,1,0:T(8,128)(2,1)}), bf16[16,72,128]{2,1,0:T(8,128)(2,1)S(1)}, u32[]{:S(2)}, u32[]{:S(2)}) async-start(bf16[16,72,128]{2,1,0:T(8,128)(2,1)} %copy.106), calls=%async_computation.4 | async-start | bytes 589824 | tf_op jit(solution)/shard_map/all_to_all | solution.py:31
  139.1 12.2 %all-to-all-done.4 = bf16[16,72,128]{2,1,0:T(8,128)(2,1)S(1)} async-done(((bf16[16,72,128]{2,1,0:T(8,128)(2,1)}), bf16[16,72,128]{2,1,0:T(8,128)(2,1)S(1)}, u32[]{:S(2)}, u32[]{:S(2)}) %all-to-all-start.4) | async-done | bytes 294944 | tf_op jit(solution)/shard_map/all_to_all | solution.py:31
  151.4 0.2 reduce_sum.45
  151.9 0.1 div.32
  152.3 15.8 %all_to_all.31.got_ref = bf16[16,80,128]{2,1,0:T(8,128)(2,1)S(1)} all-to-all(bf16[16,80,128]{2,1,0:T(8,128)(2,1)S(1)} %broadcast_in_dim.11), channel_id=1, replica_groups=mesh['y'=8,'x'=8,'z'=8,'core'=2] {'z','core'}, dimensions={0} | all-to-all | bytes 655360 | tf_op jit(solution)/shard_map/all_to_all | solution.py:31
  168.1 1.0 last_step.1
  (83 shorter events, 3.2 us)
Async XLA Ops:
  0.6 17.7 %copy-start = (bf16[512,384]{1,0:T(8,128)(2,1)S(1)}, bf16[512,384]{1,0:T(8,128)(2,1)}, u32[]{:S(2)}) copy-start(bf16[512,384]{1,0:T(8,128)(2,1)} %param.19) | copy-start | bytes 1179652
  0.6 17.2 %copy-start.2 = (bf16[512,384]{1,0:T(8,128)(2,1)S(1)}, bf16[512,384]{1,0:T(8,128)(2,1)}, u32[]{:S(2)}) copy-start(bf16[512,384]{1,0:T(8,128)(2,1)} %lift_hbm.1) | copy-start | bytes 1179652
  0.7 16.9 %copy-start.12 = (s32[384]{0:T(512)S(1)}, s32[384]{0:T(512)}, u32[]{:S(2)}) copy-start(s32[384]{0:T(512)} %param.25) | copy-start | bytes 4612
  0.7 16.9 %copy-start.11 = (s32[384]{0:T(512)S(1)}, s32[384]{0:T(512)}, u32[]{:S(2)}) copy-start(s32[384]{0:T(512)} %param.26) | copy-start | bytes 4612
  0.7 17.2 %copy-start.6 = (bf16[256,512]{1,0:T(8,128)(2,1)S(1)}, bf16[256,512]{1,0:T(8,128)(2,1)}, u32[]{:S(2)}) copy-start(bf16[256,512]{1,0:T(8,128)(2,1)} %param.18) | copy-start | bytes 786436
  0.7 17.2 %copy-start.9 = (f32[384]{0:T(512)S(1)}, f32[384]{0:T(512)}, u32[]{:S(2)}) copy-start(f32[384]{0:T(512)} %param.24) | copy-start | bytes 4612
  0.7 17.7 %copy-start.7 = (bf16[256,512]{1,0:T(8,128)(2,1)S(1)}, bf16[256,512]{1,0:T(8,128)(2,1)}, u32[]{:S(2)}) copy-start(bf16[256,512]{1,0:T(8,128)(2,1)} %param.17) | copy-start | bytes 786436
  0.7 17.7 %copy-start.10 = (f32[384]{0:T(512)S(1)}, f32[384]{0:T(512)}, u32[]{:S(2)}) copy-start(f32[384]{0:T(512)} %param.23) | copy-start | bytes 4612
  3.3 27.6 %all-to-all-start = ((bf16[64,24,128]{2,1,0:T(8,128)(2,1)}), bf16[64,24,128]{2,1,0:T(8,128)(2,1)S(1)}, u32[]{:S(2)}, u32[]{:S(2)}) async-start(bf16[64,24,128]{2,1,0:T(8,128)(2,1)} %first_step.1), calls=%async_computation | async-start | bytes 786432 | tf_op jit(solution)/shard_map/all_to_all | solution.py:31
  31.9 18.6 %copy-start.3 = (bf16[256,384]{1,0:T(8,128)(2,1)S(1)}, bf16[256,384]{1,0:T(8,128)(2,1)}, u32[]{:S(2)}) copy-start(bf16[256,384]{1,0:T(8,128)(2,1)} %top_hbm.1) | copy-start | bytes 589828
  32.0 18.6 %copy-start.5 = (bf16[384,512]{1,0:T(8,128)(2,1)S(1)}, bf16[384,512]{1,0:T(8,128)(2,1)}, u32[]{:S(2)}) copy-start(bf16[384,512]{1,0:T(8,128)(2,1)} %param.22) | copy-start | bytes 1179652
  50.6 0.9 copy-start.4
  53.3 18.9 %all-to-all-start.2 = ((bf16[64,7,4,128]{3,2,1,0:T(4,128)(2,1)}), bf16[64,7,4,128]{3,2,1,0:T(4,128)(2,1)S(1)}, u32[]{:S(2)}, u32[]{:S(2)}) async-start(bf16[64,7,4,128]{3,2,1,0:T(4,128)(2,1)} %copy.91), calls=%async_computation.2 | async-start | bytes 917504 | tf_op jit(solution)/shard_map/all_to_all | solution.py:31
  58.0 17.0 %collective-permute-start = (bf16[18,32,128]{2,1,0:T(8,128)(2,1)S(1)}, bf16[18,32,128]{2,1,0:T(8,128)(2,1)S(1)}, u32[]{:S(2)}, u32[]{:S(2)}) collective-permute-start(bf16[18,32,128]{2,1,0:T(8,128)(2,1)S(1)} %bitcast.91), channel_id=1, source_target_pairs={{0,4},{2,6},{4,0},{6,2},{8,12},{10,14},{12,8},{14,10},{1,5},{3,7},... | collective-permute-start | bytes 442376 | tf_op jit(solution)/shard_map/ppermute | solution.py:189
  78.5 29.9 %all-to-all-start.3 = ((bf16[64,13,4,128]{3,2,1,0:T(4,128)(2,1)}), bf16[64,13,4,128]{3,2,1,0:T(4,128)(2,1)S(1)}, u32[]{:S(2)}, u32[]{:S(2)}) async-start(bf16[64,13,4,128]{3,2,1,0:T(4,128)(2,1)} %copy.97), calls=%async_computation.3 | async-start | bytes 1703936 | tf_op jit(solution)/shard_map/all_to_all | solution.py:31
  92.3 17.7 %collective-permute-start.1 = (bf16[1152,128]{1,0:T(8,128)(2,1)S(1)}, bf16[1152,128]{1,0:T(8,128)(2,1)S(1)}, u32[]{:S(2)}, u32[]{:S(2)}) collective-permute-start(bf16[1152,128]{1,0:T(8,128)(2,1)S(1)} %bitcast.94), channel_id=1, source_target_pairs={{0,1},{1,0},{2,3},{3,2},{4,5},{5,4},{6,7},{7,6},{8,9},{9,8},{10,11... | collective-permute-start | bytes 884744 | tf_op jit(solution)/shard_map/ppermute | solution.py:207
  101.0 10.5 %collective-permute-start.2 = (bf16[1152,128]{1,0:T(8,128)(2,1)S(1)}, bf16[1152,128]{1,0:T(8,128)(2,1)S(1)}, u32[]{:S(2)}, u32[]{:S(2)}) collective-permute-start(bf16[1152,128]{1,0:T(8,128)(2,1)S(1)} %bitcast.95), channel_id=1, source_target_pairs={{0,2},{1,3},{2,0},{3,1},{4,6},{5,7},{6,4},{7,5},{8,10},{9,11},{10,... | collective-permute-start | bytes 884744 | tf_op jit(solution)/shard_map/ppermute | solution.py:207
  102.9 15.1 %collective-permute-start.3 = (bf16[1152,128]{1,0:T(8,128)(2,1)S(1)}, bf16[1152,128]{1,0:T(8,128)(2,1)}, u32[]{:S(2)}, u32[]{:S(2)}) collective-permute-start(bf16[1152,128]{1,0:T(8,128)(2,1)S(1)} %bitcast.96), channel_id=1, source_target_pairs={{0,3},{1,2},{2,1},{3,0},{4,7},{5,6},{6,5},{7,4},{8,11},{9,10},{10,... | collective-permute-start | bytes 884744 | tf_op jit(solution)/shard_map/ppermute | solution.py:207
  119.8 19.1 %copy-start.8 = (f32[18,128]{1,0:T(8,128)S(1)}, f32[18,128]{1,0:T(8,128)}, u32[]{:S(2)}) copy-start(f32[18,128]{1,0:T(8,128)} %param.29) | copy-start | bytes 27652
  120.5 47.6 %copy-start.1 = (f32[18,8192]{1,0:T(8,128)S(1)}, f32[18,8192]{1,0:T(8,128)}, u32[]{:S(2)}) copy-start(f32[18,8192]{1,0:T(8,128)} %rows_ref.1) | copy-start | bytes 1769476
  121.3 30.0 %all-to-all-start.4 = ((bf16[16,72,128]{2,1,0:T(8,128)(2,1)}), bf16[16,72,128]{2,1,0:T(8,128)(2,1)S(1)}, u32[]{:S(2)}, u32[]{:S(2)}) async-start(bf16[16,72,128]{2,1,0:T(8,128)(2,1)} %copy.106), calls=%async_computation.4 | async-start | bytes 589824 | tf_op jit(solution)/shard_map/all_to_all | solution.py:31

commit v5 on v4

--- a/solution.py
+++ b/solution.py
@@ -205,12 +205,10 @@
     send, part = lax.optimization_barrier((send, part))
     got = move(send)
     parts = [part] + [lax.ppermute(part, REP, [(i, i ^ k) for i in range(N_REP)]) for k in (1, 2, 3)]
+    for bit in (1, 2):
+        parts = [jnp.where(quarter & bit == 0, parts[k], parts[k ^ bit]) for k in range(4)]
     squeeze_own = jnp.concatenate(parts, axis=1)
-    tiles = got[:, :16].reshape(16, 4, 16, 128)
-    blocks = [tiles[:, k] for k in range(4)]
-    for bit in (1, 2):
-        blocks = [jnp.where(quarter & bit == 0, blocks[k], blocks[k ^ bit]) for k in range(4)]
-    rank_zero = jnp.concatenate([block.reshape(ROWS, 128) for block in blocks], axis=1)
+    rank_zero = from_tiles(got[:, :16])
     pooled_slots = (
         got[:, 16:].reshape(EMB, 2, SLOT_MAX, 128).transpose(2, 0, 1, 3).reshape(SLOT_MAX * EMB, ROWS)
     )

time: 170 us -> 169 us (level)
  starting transfers between devices: 76.6 us -> 74.6 us
  other arithmetic: 3.66 us -> 5.6 us
    all_to_all x4, starting transfers between devices: 48.1 us -> 46.1 us  [exchange(): return lax.all_to_all(blocks, axis, split_axis=0, concat_axis=0, tiled=True)]
    select_n x2 -> x1, other arithmetic: 0.18 us -> 2.12 us  [shards(): jnp.where(quarter & bit == 0, parts[k], parts[k ^ bit])]
    all_to_all x4, waiting for transfers between devices: 25.8 us -> 24 us  [exchange(): return lax.all_to_all(blocks, axis, split_axis=0, concat_axis=0, tiled=True)]
  transfers between devices with their start and end apart: 8 -> 8, of which waited for: 6 -> 5; matrix products, arithmetic and copies ran while one was open for 3% -> 4% of each run, Pallas kernels for 0% -> 0%
where the time goes in v5:
time: 169 us; the launch traced here: 168 us
  starting transfers between devices  74.6 us (44%)
  waiting for transfers between devices  36.3 us (21%)
  blocking collectives  34.1 us (20%)
  local copies, waits for them, and re-layouts  9.2 us (5%)
  other arithmetic  5.6 us (3%)
  Pallas kernels  3.56 us (2%)
  matrix products  3.18 us (2%)
    all_to_all x4, starting transfers between devices, exchange(): return lax.all_to_all(blocks, axis, split_axis=0, concat_axis=0, tiled=True)  46.1 us
    all_to_all x2, blocking collectives, exchange(): return lax.all_to_all(blocks, axis, split_axis=0, concat_axis=0, tiled=True)  34.1 us
    all_to_all x4, waiting for transfers between devices, exchange(): return lax.all_to_all(blocks, axis, split_axis=0, concat_axis=0, tiled=True)  24 us
    ppermute x3, starting transfers between devices, shards(): lax.ppermute(part, REP, [(i, i ^ k) for i in range(N_REP)])  14.3 us
    ppermute x1, starting transfers between devices, shards(): other = lax.ppermute(part, 'z', [(i, i ^ 2) for i in range(8)])  14.2 us
    ppermute x3, waiting for transfers between devices, shards(): lax.ppermute(part, REP, [(i, i ^ k) for i in range(N_REP)])  9.63 us
  transfers between devices with their start and end apart: 8, of which 5 were waited for; matrix products, arithmetic and copies ran while one was open for 4% of the time, Pallas kernels for 0%

profile of v5, /device:TPU:1, one launch (start us, length us, event | category | flops | bytes accessed | tf_op | source)
XLA Modules:
  0.0 168.0 jit_solution(5766896162578579505)
XLA Ops:
  0.7 2.5 %first_step.1 = bf16[64,24,128]{2,1,0:T(8,128)(2,1)} custom-call(bf16[256,384]{1,0:T(8,128)(2,1)} %x_hbm.1, bf16[256,384]{1,0:T(8,128)(2,1)} %top_hbm.1, bf16[512,384]{1,0:T(8,128)(2,1)} %lift_hbm.1, bf16[384,512]{1,0:T(8,128)(2,1)} %squeeze_hbm.1), custom_call_target="tpu_custom_call" | custom-call | tf_op jit(solution)/shard_map/first_step/pallas_call | solution.py:83
  3.3 14.0 %all-to-all-start = ((bf16[64,24,128]{2,1,0:T(8,128)(2,1)}), bf16[64,24,128]{2,1,0:T(8,128)(2,1)S(1)}, u32[]{:S(2)}, u32[]{:S(2)}) async-start(bf16[64,24,128]{2,1,0:T(8,128)(2,1)} %first_step.1), calls=%async_computation | async-start | bytes 786432 | tf_op jit(solution)/shard_map/all_to_all | solution.py:31
  17.4 0.1 add.124
  17.6 0.1 reshape.146
  17.9 0.3 convolution_add_fusion.3
  18.2 0.2 compare_convert_fusion
  18.4 0.3 convolution_add_fusion.2
  18.7 0.3 fusion.1
  19.1 11.8 %all-to-all-done = bf16[64,24,128]{2,1,0:T(8,128)(2,1)S(1)} async-done(((bf16[64,24,128]{2,1,0:T(8,128)(2,1)}), bf16[64,24,128]{2,1,0:T(8,128)(2,1)S(1)}, u32[]{:S(2)}, u32[]{:S(2)}) %all-to-all-start) | async-done | bytes 393248 | tf_op jit(solution)/shard_map/all_to_all | solution.py:31
  30.9 0.3 convolution_convert_fusion.4
  31.6 0.4 copy.61
  32.0 18.3 %all_to_all.30 = bf16[64,7,4,128]{3,2,1,0:T(4,128)(2,1)S(1)} all-to-all(bf16[64,7,4,128]{3,2,1,0:T(4,128)(2,1)S(1)} %copy.61), channel_id=1, replica_groups=mesh['y'=8,'x'=8,'z'=8,'core'=2] {'y','x'}, dimensions={0} | all-to-all | bytes 917504 | tf_op jit(solution)/shard_map/all_to_all | solution.py:31
  50.6 0.3 fusion.12
  50.9 0.1 copy.65
  51.1 0.1 copy.67
  51.3 0.2 copy-done.4
  51.5 0.3 convolution_convert_fusion.3
  52.0 0.2 copy.68
  52.2 1.1 copy.69
  53.3 4.6 %all-to-all-start.2 = ((bf16[64,7,4,128]{3,2,1,0:T(4,128)(2,1)}), bf16[64,7,4,128]{3,2,1,0:T(4,128)(2,1)S(1)}, u32[]{:S(2)}, u32[]{:S(2)}) async-start(bf16[64,7,4,128]{3,2,1,0:T(4,128)(2,1)} %copy.69), calls=%async_computation.2 | async-start | bytes 917504 | tf_op jit(solution)/shard_map/all_to_all | solution.py:31
  58.0 14.2 %collective-permute-start = (bf16[18,32,128]{2,1,0:T(8,128)(2,1)S(1)}, bf16[18,32,128]{2,1,0:T(8,128)(2,1)S(1)}, u32[]{:S(2)}, u32[]{:S(2)}) collective-permute-start(bf16[18,32,128]{2,1,0:T(8,128)(2,1)S(1)} %bitcast.97), channel_id=1, source_target_pairs={{0,4},{2,6},{4,0},{6,2},{8,12},{10,14},{12,8},{14,10},{1,5},{3,7},... | collective-permute-start | bytes 442376 | tf_op jit(solution)/shard_map/ppermute | solution.py:189
  72.3 2.7 %collective-permute-done = bf16[18,32,128]{2,1,0:T(8,128)(2,1)S(1)} collective-permute-done((bf16[18,32,128]{2,1,0:T(8,128)(2,1)S(1)}, bf16[18,32,128]{2,1,0:T(8,128)(2,1)S(1)}, u32[]{:S(2)}, u32[]{:S(2)}) %collective-permute-start) | collective-permute-done | bytes 147488 | tf_op jit(solution)/shard_map/ppermute | solution.py:189
  75.2 0.4 convolution_convert_fusion.1
  75.8 0.4 convolution_convert_fusion
  76.4 0.2 pad_maximum_fusion
  76.6 0.2 copy.74
  76.9 1.6 copy.75
  78.5 11.8 %all-to-all-start.3 = ((bf16[64,13,4,128]{3,2,1,0:T(4,128)(2,1)}), bf16[64,13,4,128]{3,2,1,0:T(4,128)(2,1)S(1)}, u32[]{:S(2)}, u32[]{:S(2)}) async-start(bf16[64,13,4,128]{3,2,1,0:T(4,128)(2,1)} %copy.75), calls=%async_computation.3 | async-start | bytes 1703936 | tf_op jit(solution)/shard_map/all_to_all | solution.py:31
  90.3 8.7 %collective-permute-start.1 = (bf16[1152,128]{1,0:T(8,128)(2,1)S(1)}, bf16[1152,128]{1,0:T(8,128)(2,1)S(1)}, u32[]{:S(2)}, u32[]{:S(2)}) collective-permute-start(bf16[1152,128]{1,0:T(8,128)(2,1)S(1)} %bitcast.85), channel_id=1, source_target_pairs={{0,1},{1,0},{2,3},{3,2},{4,5},{5,4},{6,7},{7,6},{8,9},{9,8},{10,11... | collective-permute-start | bytes 884744 | tf_op jit(solution)/shard_map/ppermute | solution.py:207
  99.0 1.9 %collective-permute-start.2 = (bf16[1152,128]{1,0:T(8,128)(2,1)S(1)}, bf16[1152,128]{1,0:T(8,128)(2,1)S(1)}, u32[]{:S(2)}, u32[]{:S(2)}) collective-permute-start(bf16[1152,128]{1,0:T(8,128)(2,1)S(1)} %bitcast.86), channel_id=1, source_target_pairs={{0,2},{1,3},{2,0},{3,1},{4,6},{5,7},{6,4},{7,5},{8,10},{9,11},{10,... | collective-permute-start | bytes 884744 | tf_op jit(solution)/shard_map/ppermute | solution.py:207
  101.0 3.7 %collective-permute-start.3 = (bf16[1152,128]{1,0:T(8,128)(2,1)S(1)}, bf16[1152,128]{1,0:T(8,128)(2,1)}, u32[]{:S(2)}, u32[]{:S(2)}) collective-permute-start(bf16[1152,128]{1,0:T(8,128)(2,1)S(1)} %bitcast.87), channel_id=1, source_target_pairs={{0,3},{1,2},{2,1},{3,0},{4,7},{5,6},{6,5},{7,4},{8,11},{9,10},{10,... | collective-permute-start | bytes 884744 | tf_op jit(solution)/shard_map/ppermute | solution.py:207
  104.7 1.9 %convert_element_type.75 = bf16[18,256,128]{2,1,0:T(8,128)(2,1)S(1)} convert(s32[18,256,128]{2,1,0:T(8,128)} %param.27) | non-fusion elementwise | flops 589824 | bytes 3538944 | tf_op jit(solution)/shard_map/convert_element_type | solution.py:162
  106.6 2.9 %collective-permute-done.2 = bf16[1152,128]{1,0:T(8,128)(2,1)S(1)} collective-permute-done((bf16[1152,128]{1,0:T(8,128)(2,1)S(1)}, bf16[1152,128]{1,0:T(8,128)(2,1)S(1)}, u32[]{:S(2)}, u32[]{:S(2)}) %collective-permute-start.2) | collective-permute-done | bytes 294944 | tf_op jit(solution)/shard_map/ppermute | solution.py:207
  109.5 6.7 %collective-permute-done.3 = bf16[1152,128]{1,0:T(8,128)(2,1)} collective-permute-done((bf16[1152,128]{1,0:T(8,128)(2,1)S(1)}, bf16[1152,128]{1,0:T(8,128)(2,1)}, u32[]{:S(2)}, u32[]{:S(2)}) %collective-permute-start.3) | collective-permute-done | bytes 294944 | tf_op jit(solution)/shard_map/ppermute | solution.py:207
  116.3 2.1 %broadcast_select_fusion.7 = (bf16[1152,128]{1,0:T(8,128)(2,1)}, bf16[1152,128]{1,0:T(8,128)(2,1)}, bf16[1152,128]{1,0:T(8,128)(2,1)}, bf16[1152,128]{1,0:T(8,128)(2,1)}) fusion(pred[]{:T(512)S(6)} %eq.55, bf16[1152,128]{1,0:T(8,128)(2,1)S(1)} %bitcast.88, bf16[1152,128]{1,0:T(8,128)(2,1)S(1)} %collective-permute-done.1, pred[]{:T(512)S(6)} %eq.56, ...), kind=kLoop, calls=%fused_computation.39 | loop fusion | flops 1179648 | bytes 2359298 | tf_op jit(solution)/shard_map/jit(_where)/select_n | solution.py:209
  118.4 0.2 copy.76
  118.7 0.6 copy.77
  119.9 0.5 fusion
  120.4 0.3 fusion.9
  120.8 0.3 copy.79
  121.1 0.3 reshape.172
  121.4 0.8 copy.81
  122.2 15.6 %all-to-all-start.4 = ((bf16[16,72,128]{2,1,0:T(8,128)(2,1)}), bf16[16,72,128]{2,1,0:T(8,128)(2,1)S(1)}, u32[]{:S(2)}, u32[]{:S(2)}) async-start(bf16[16,72,128]{2,1,0:T(8,128)(2,1)} %copy.81), calls=%async_computation.4 | async-start | bytes 589824 | tf_op jit(solution)/shard_map/all_to_all | solution.py:31
  138.0 12.2 %all-to-all-done.4 = bf16[16,72,128]{2,1,0:T(8,128)(2,1)S(1)} async-done(((bf16[16,72,128]{2,1,0:T(8,128)(2,1)}), bf16[16,72,128]{2,1,0:T(8,128)(2,1)S(1)}, u32[]{:S(2)}, u32[]{:S(2)}) %all-to-all-start.4) | async-done | bytes 294944 | tf_op jit(solution)/shard_map/all_to_all | solution.py:31
  150.4 0.2 reduce_sum.45
  150.8 0.1 div.32
  151.2 15.8 %all_to_all.31.got_ref = bf16[16,80,128]{2,1,0:T(8,128)(2,1)S(1)} all-to-all(bf16[16,80,128]{2,1,0:T(8,128)(2,1)S(1)} %broadcast_in_dim.11), channel_id=1, replica_groups=mesh['y'=8,'x'=8,'z'=8,'core'=2] {'z','core'}, dimensions={0} | all-to-all | bytes 655360 | tf_op jit(solution)/shard_map/all_to_all | solution.py:31
  167.0 1.0 last_step.1
  (90 shorter events, 3.4 us)
Async XLA Ops:
  0.6 17.7 %copy-start = (bf16[512,384]{1,0:T(8,128)(2,1)S(1)}, bf16[512,384]{1,0:T(8,128)(2,1)}, u32[]{:S(2)}) copy-start(bf16[512,384]{1,0:T(8,128)(2,1)} %param.19) | copy-start | bytes 1179652
  0.6 17.2 %copy-start.2 = (bf16[512,384]{1,0:T(8,128)(2,1)S(1)}, bf16[512,384]{1,0:T(8,128)(2,1)}, u32[]{:S(2)}) copy-start(bf16[512,384]{1,0:T(8,128)(2,1)} %lift_hbm.1) | copy-start | bytes 1179652
  0.7 16.9 %copy-start.16 = (s32[384]{0:T(512)S(1)}, s32[384]{0:T(512)}, u32[]{:S(2)}) copy-start(s32[384]{0:T(512)} %param.25) | copy-start | bytes 4612
  0.7 16.9 %copy-start.15 = (s32[384]{0:T(512)S(1)}, s32[384]{0:T(512)}, u32[]{:S(2)}) copy-start(s32[384]{0:T(512)} %param.26) | copy-start | bytes 4612
  0.7 17.2 %copy-start.10 = (bf16[256,512]{1,0:T(8,128)(2,1)S(1)}, bf16[256,512]{1,0:T(8,128)(2,1)}, u32[]{:S(2)}) copy-start(bf16[256,512]{1,0:T(8,128)(2,1)} %param.18) | copy-start | bytes 786436
  0.7 17.2 %copy-start.13 = (f32[384]{0:T(512)S(1)}, f32[384]{0:T(512)}, u32[]{:S(2)}) copy-start(f32[384]{0:T(512)} %param.24) | copy-start | bytes 4612
  0.7 17.7 %copy-start.11 = (bf16[256,512]{1,0:T(8,128)(2,1)S(1)}, bf16[256,512]{1,0:T(8,128)(2,1)}, u32[]{:S(2)}) copy-start(bf16[256,512]{1,0:T(8,128)(2,1)} %param.17) | copy-start | bytes 786436
  0.7 17.7 %copy-start.14 = (f32[384]{0:T(512)S(1)}, f32[384]{0:T(512)}, u32[]{:S(2)}) copy-start(f32[384]{0:T(512)} %param.23) | copy-start | bytes 4612
  3.3 27.6 %all-to-all-start = ((bf16[64,24,128]{2,1,0:T(8,128)(2,1)}), bf16[64,24,128]{2,1,0:T(8,128)(2,1)S(1)}, u32[]{:S(2)}, u32[]{:S(2)}) async-start(bf16[64,24,128]{2,1,0:T(8,128)(2,1)} %first_step.1), calls=%async_computation | async-start | bytes 786432 | tf_op jit(solution)/shard_map/all_to_all | solution.py:31
  31.9 18.6 %copy-start.3 = (bf16[256,384]{1,0:T(8,128)(2,1)S(1)}, bf16[256,384]{1,0:T(8,128)(2,1)}, u32[]{:S(2)}) copy-start(bf16[256,384]{1,0:T(8,128)(2,1)} %top_hbm.1) | copy-start | bytes 589828
  32.0 18.6 %copy-start.5 = (bf16[384,512]{1,0:T(8,128)(2,1)S(1)}, bf16[384,512]{1,0:T(8,128)(2,1)}, u32[]{:S(2)}) copy-start(bf16[384,512]{1,0:T(8,128)(2,1)} %param.22) | copy-start | bytes 1179652
  50.6 0.9 copy-start.4
  53.3 18.9 %all-to-all-start.2 = ((bf16[64,7,4,128]{3,2,1,0:T(4,128)(2,1)}), bf16[64,7,4,128]{3,2,1,0:T(4,128)(2,1)S(1)}, u32[]{:S(2)}, u32[]{:S(2)}) async-start(bf16[64,7,4,128]{3,2,1,0:T(4,128)(2,1)} %copy.69), calls=%async_computation.2 | async-start | bytes 917504 | tf_op jit(solution)/shard_map/all_to_all | solution.py:31
  58.0 17.0 %collective-permute-start = (bf16[18,32,128]{2,1,0:T(8,128)(2,1)S(1)}, bf16[18,32,128]{2,1,0:T(8,128)(2,1)S(1)}, u32[]{:S(2)}, u32[]{:S(2)}) collective-permute-start(bf16[18,32,128]{2,1,0:T(8,128)(2,1)S(1)} %bitcast.97), channel_id=1, source_target_pairs={{0,4},{2,6},{4,0},{6,2},{8,12},{10,14},{12,8},{14,10},{1,5},{3,7},... | collective-permute-start | bytes 442376 | tf_op jit(solution)/shard_map/ppermute | solution.py:189
  78.5 39.9 %all-to-all-start.3 = ((bf16[64,13,4,128]{3,2,1,0:T(4,128)(2,1)}), bf16[64,13,4,128]{3,2,1,0:T(4,128)(2,1)S(1)}, u32[]{:S(2)}, u32[]{:S(2)}) async-start(bf16[64,13,4,128]{3,2,1,0:T(4,128)(2,1)} %copy.75), calls=%async_computation.3 | async-start | bytes 1703936 | tf_op jit(solution)/shard_map/all_to_all | solution.py:31
  90.3 16.3 %collective-permute-start.1 = (bf16[1152,128]{1,0:T(8,128)(2,1)S(1)}, bf16[1152,128]{1,0:T(8,128)(2,1)S(1)}, u32[]{:S(2)}, u32[]{:S(2)}) collective-permute-start(bf16[1152,128]{1,0:T(8,128)(2,1)S(1)} %bitcast.85), channel_id=1, source_target_pairs={{0,1},{1,0},{2,3},{3,2},{4,5},{5,4},{6,7},{7,6},{8,9},{9,8},{10,11... | collective-permute-start | bytes 884744 | tf_op jit(solution)/shard_map/ppermute | solution.py:207
  99.0 10.5 %collective-permute-start.2 = (bf16[1152,128]{1,0:T(8,128)(2,1)S(1)}, bf16[1152,128]{1,0:T(8,128)(2,1)S(1)}, u32[]{:S(2)}, u32[]{:S(2)}) collective-permute-start(bf16[1152,128]{1,0:T(8,128)(2,1)S(1)} %bitcast.86), channel_id=1, source_target_pairs={{0,2},{1,3},{2,0},{3,1},{4,6},{5,7},{6,4},{7,5},{8,10},{9,11},{10,... | collective-permute-start | bytes 884744 | tf_op jit(solution)/shard_map/ppermute | solution.py:207
  101.0 15.3 %collective-permute-start.3 = (bf16[1152,128]{1,0:T(8,128)(2,1)S(1)}, bf16[1152,128]{1,0:T(8,128)(2,1)}, u32[]{:S(2)}, u32[]{:S(2)}) collective-permute-start(bf16[1152,128]{1,0:T(8,128)(2,1)S(1)} %bitcast.87), channel_id=1, source_target_pairs={{0,3},{1,2},{2,1},{3,0},{4,7},{5,6},{6,5},{7,4},{8,11},{9,10},{10,... | collective-permute-start | bytes 884744 | tf_op jit(solution)/shard_map/ppermute | solution.py:207
  118.7 1.0 copy-start.6
  118.7 1.0 copy-start.7
  118.7 1.1 copy-start.8
  118.7 1.2 copy-start.9
  120.7 17.1 %copy-start.12 = (f32[18,128]{1,0:T(8,128)S(1)}, f32[18,128]{1,0:T(8,128)}, u32[]{:S(2)}) copy-start(f32[18,128]{1,0:T(8,128)} %param.29) | copy-start | bytes 27652
  121.4 45.6 %copy-start.1 = (f32[18,8192]{1,0:T(8,128)S(1)}, f32[18,8192]{1,0:T(8,128)}, u32[]{:S(2)}) copy-start(f32[18,8192]{1,0:T(8,128)} %rows_ref.1) | copy-start | bytes 1769476
  122.2 28.0 %all-to-all-start.4 = ((bf16[16,72,128]{2,1,0:T(8,128)(2,1)}), bf16[16,72,128]{2,1,0:T(8,128)(2,1)S(1)}, u32[]{:S(2)}, u32[]{:S(2)}) async-start(bf16[16,72,128]{2,1,0:T(8,128)(2,1)} %copy.81), calls=%async_computation.4 | async-start | bytes 589824 | tf_op jit(solution)/shard_map/all_to_all | solution.py:31
